TPU v7x, 256 devices: a whole 4x4x8 slice. The times are simulated.
256 devices in a mesh: section: 2 (over y_lo), fsdp: 32 (over z, y_hi, core), seq: 4 (over x).
Axes of the slice: x: 4, y: 4 (y_hi: 2, y_lo: 2; y = y_hi * 2 + y_lo), z: 8, core: 2. Of those that a mesh axis runs over, the one named last changes fastest.
Arguments:
- inputs: bfloat16 [2, 4, 6144, 4096], P('section', None, 'fsdp', 'seq'), may hold values from -6 to 6
- gains: float32 [2, 4096], P('section'), may hold values from 0.25 to 1.75
- weights: bfloat16 [2, 4096, 2, 4096], P('section', 'fsdp', None, 'seq'), may hold values from -0.09375 to 0.09375
- lengths: int32 [4, 32], P(None, 'fsdp'), may hold values from 1 to 192
Outputs:
- section_outputs: bfloat16 [2, 4, 6144, 2, 4096], P('section', None, 'fsdp', None, 'seq')
All inputs are finite; a program needn't handle non-finite values.
Results may differ from a plain program's by a relative error of at most 0.005.
Values may be sent and summed in bfloat16 or wider, within the bound.
No kernel may reach another device: no remote copies, remote signals or barrier semaphores. Data moves between devices by JAX's collectives and lax.ppermute only.
A program may use at most 128 MiB of HBM per device.

v0:
```python
import jax
import jax.numpy as jnp
from jax import lax
from jax.sharding import PartitionSpec as P

HD = 64


def passed_along(x, axis, by):
    size = lax.axis_size(axis)
    pairs = [(i, i + by) for i in range(size) if 0 <= i + by < size]
    return lax.ppermute(x, axis, pairs)


def attend(proj_dec, proj_enc, limit, head_dim):
    batch, tok, _, width = proj_dec.shape
    heads = width // head_dim
    query = proj_dec[:, :, 0].reshape(batch, tok, heads, head_dim)
    gate = proj_dec[:, :, 1]
    key = proj_enc[:, :, 0].reshape(batch, tok, heads, head_dim)
    value = proj_enc[:, :, 1].reshape(batch, tok, heads, head_dim)
    scores = jnp.einsum(
        "mqhe,mkhe->mhqk", query, key, preferred_element_type=jnp.float32
    ) / jnp.sqrt(jnp.float32(head_dim))
    place = jnp.arange(tok, dtype=jnp.int32)
    valid = place[None, None, None, :] < limit[:, None, None, None]
    scores = jnp.where(valid, scores, jnp.float32(-1e30))
    probs = jax.nn.softmax(scores, axis=-1).astype(jnp.bfloat16)
    context = jnp.einsum("mhqk,mkhe->mqhe", probs, value, preferred_element_type=jnp.float32)
    context = context.reshape(batch, tok, width)
    return (jax.nn.sigmoid(gate.astype(jnp.float32)) * context).astype(jnp.bfloat16)


def per_device(inputs, gains, weights, lengths):
    whole = lax.all_gather(inputs, "seq", axis=3, tiled=True)[0]
    batch, tok, width = whole.shape
    local_width = weights.shape[3]
    values = whole.astype(jnp.float32)
    mean_sq = jnp.mean(values * values, axis=-1, keepdims=True)
    normed = (values * lax.rsqrt(mean_sq + 1e-06) * gains[0][None, None, :]).astype(jnp.bfloat16)
    rows = normed.reshape(batch * tok, width)
    full = lax.all_gather(weights, "fsdp", axis=1, tiled=True)[0]
    proj = jnp.dot(rows, full.reshape(width, 2 * local_width), preferred_element_type=jnp.float32)
    projected = proj.astype(jnp.bfloat16).reshape(batch, tok, 2, local_width)
    limit = lengths[:, 0]
    is_decoder = lax.axis_index("section") == 1
    memory = passed_along(projected, "section", 1)
    attended = lax.cond(
        is_decoder,
        lambda: attend(projected, memory, limit, HD),
        lambda: jnp.zeros((projected.shape[0], tok, local_width), jnp.bfloat16),
    )
    first = jnp.where(is_decoder, attended, projected[:, :, 0])
    final = jnp.stack([first, projected[:, :, 1]], axis=2)
    return final[None]


def solution(mesh):
    in_specs = (
        P("section", None, "fsdp", "seq"),
        P("section", None),
        P("section", "fsdp", None, "seq"),
        P(None, "fsdp"),
    )
    out_specs = P("section", None, "fsdp", None, "seq")
    return jax.shard_map(
        per_device, mesh=mesh, in_specs=in_specs, out_specs=out_specs, check_vma=False
    )
```

profile of v0, /device:TPU:8, one launch (start us, length us, event | category | flops | bytes accessed | tf_op | source)
XLA Modules:
  0.0 382.8 jit_solution(13446876624266932745)
XLA Ops:
  6.5 0.0 copy-start.4
  6.5 0.0 all-gather.3.cloned.1.call-start
  6.5 0.7 all-gather.3.cloned.1.call-update
  7.3 0.0 all-gather.5.cloned.1.call-start
  7.3 0.7 all-gather.5.cloned.1.call-update
  8.0 72.3 %all-gather.3.cloned.1.call-done = bf16[1,4,192,4096]{3,2,1,0:T(8,128)(2,1)} async-done(((bf16[1,4,192,1024]{3,2,1,0:T(8,128)(2,1)}), bf16[1,4,192,4096]{3,2,1,0:T(8,128)(2,1)}) %all-gather.3.cloned.1.call-update) | async-done | bytes 6291472 | tf_op jit(solution)/shard_map/all_gather | solution.py:35
  80.3 0.0 copy-start
  80.3 4.2 %fusion.11 = f32[4,192]{1,0:T(4,128)S(1)} fusion(bf16[1,4,192,4096]{3,2,1,0:T(8,128)(2,1)} %all-gather.3.cloned.1.call-done), kind=kLoop, calls=%fused_computation.17 | loop fusion | flops 9436416 | bytes 6294528 | tf_op jit(solution)/shard_map/reduce_sum | solution.py:39
  84.5 0.0 copy-done.4
  84.5 0.3 copy-done
  84.9 5.4 %fusion.13 = bf16[1,4,192,4096]{3,2,1,0:T(8,128)(2,1)} fusion(bf16[1,4,192,4096]{3,2,1,0:T(8,128)(2,1)S(1)} %copy-done, f32[4096]{0:T(1024)S(1)} %bitcast.43, f32[4,192]{1,0:T(4,128)S(1)} %add_rsqrt_fusion), kind=kLoop, calls=%fused_computation.19 | loop fusion | flops 12582912 | bytes 12602368 | tf_op jit(solution)/shard_map/convert_element_type | solution.py:40
  90.2 130.4 %all-gather.5.cloned.1.call-done = bf16[1,4096,2,1024]{3,2,0,1:T(2,128)(2,1)} async-done(((bf16[1,128,2,1024]{3,2,0,1:T(2,128)(2,1)}), bf16[1,4096,2,1024]{3,2,0,1:T(2,128)(2,1)}) %all-gather.5.cloned.1.call-update) | async-done | bytes 16777232 | tf_op jit(solution)/shard_map/all_gather | solution.py:42
  220.7 0.0 copy-start.2
  220.7 12.1 %copy.32 = bf16[512,8,2,1024]{3,1,2,0:T(8,128)(2,1)S(1)} copy(bf16[512,8,2,1024]{3,2,1,0:T(2,128)(2,1)} %bitcast.36) | data formatting | bytes 33554432
  232.8 0.0 copy-done.2
  232.8 14.5 %convolution_convert_fusion = bf16[768,2048]{1,0:T(8,128)(2,1)} fusion(bf16[768,4096]{1,0:T(8,128)(2,1)S(1)} %bitcast.39, bf16[4096,2048]{1,0:T(8,128)(2,1)S(1)} %bitcast.37), kind=kOutput, calls=%fused_computation.20 | convolution fusion | flops 12886474752 | bytes 26214400 | tf_op jit(solution)/shard_map/dot_general | solution.py:43
  247.3 4.8 %reshape.64 = bf16[4,192,2,1024]{3,2,1,0:T(2,128)(2,1)S(1)} reshape(bf16[768,2048]{1,0:T(8,128)(2,1)} %convolution_convert_fusion) | data formatting | bytes 6291456 | tf_op jit(solution)/shard_map/reshape | solution.py:44
  252.0 2.6 copy.20
  254.6 1.5 collective-permute-start
  256.1 5.3 %fusion.18 = (bf16[4,192,1,1024]{3,2,1,0:T(2,128)(2,1)}, bf16[4,192,1,1024]{3,2,1,0:T(2,128)(2,1)S(1)}) fusion(bf16[4,192,2,1024]{3,2,1,0:T(2,128)(2,1)S(1)} %reshape.64), kind=kLoop, calls=%fused_computation.28 | loop fusion | bytes 6291456 | tf_op jit(solution)/shard_map/slice | solution.py:53
  261.4 0.0 copy-start.5
  261.4 1.8 copy.31
  263.3 63.8 %collective-permute-done = bf16[4,192,2,1024]{3,1,2,0:T(8,128)(2,1)} collective-permute-done((bf16[4,192,2,1024]{3,1,2,0:T(8,128)(2,1)}, bf16[4,192,2,1024]{3,1,2,0:T(8,128)(2,1)}, u32[]{:S(2)}, u32[]{:S(2)}) %collective-permute-start) | collective-permute-done | bytes 3145760 | tf_op jit(solution)/shard_map/ppermute | solution.py:12
  327.1 0.0 copy-done.5
  327.1 40.7 %conditional.1 = (bf16[4,192,1024]{2,1,0:T(8,128)(2,1)}) conditional(s32[]{:T(128)} %convert_element_type.29, () %tuple.11, (bf16[4,192,2,1024]{3,2,1,0:T(2,128)(2,1)S(1)}, s32[4,1]{0,1:T(1,128)S(1)}, bf16[4,192,2,1024]{3,1,2,0:T(8,128)(2,1)}) %tuple.27), branch_computations={%region_1.0_spmd, %region_2.5_spmd} | conditional | flops 622855104 | bytes 73500232 | solution.py:48
  327.1 6.0 %copy.22 = bf16[4,192,2,1024]{1,3,0,2:T(8,128)(2,1)} copy(bf16[4,192,2,1024]{3,1,2,0:T(8,128)(2,1)} %get-tuple-element.27) | data formatting | bytes 6291456 | tf_op jit(solution)/shard_map
  333.1 4.5 %fusion.16 = (bf16[4,192,1,1024]{1,3,0,2:T(8,128)(2,1)}, bf16[4,192,1,1024]{1,3,0,2:T(8,128)(2,1)}) fusion(bf16[4,192,2,1024]{1,3,0,2:T(8,128)(2,1)} %copy.22), kind=kLoop, calls=%fused_computation.26 | loop fusion | bytes 6291456 | tf_op jit(solution)/shard_map/cond/branch_1_fun/slice | solution.py:20
  337.6 6.6 %copy.21 = bf16[4,192,2,1024]{1,3,0,2:T(8,128)(2,1)} copy(bf16[4,192,2,1024]{3,2,1,0:T(2,128)(2,1)S(1)} %get-tuple-element.25) | data formatting | bytes 6291456 | tf_op jit(solution)/shard_map
  344.2 0.0 slice-start
  344.2 0.1 iota_compare_fusion
  344.3 1.5 slice-done
  345.8 11.5 %fusion.17 = (f32[4,16,192]{2,1,0:T(8,128)S(1)}, f32[4,16,192,192]{2,3,1,0:T(8,128)}) fusion(pred[4,192]{1,0:T(4,128)(4,1)S(1)} %iota_compare_fusion, bf16[4,192,16,64]{1,3,2,0:T(8,128)(2,1)S(1)} %bitcast.38, bf16[4,192,16,64]{1,3,2,0:T(8,128)(2,1)} %bitcast.41), kind=kOutput, calls=%fused_computation.27 | convolution fusion | flops 311427264 | bytes 12632832 | tf_op jit(solution)/shard_map/cond/branch_1_fun/sub | solution.py:28
  357.3 0.0 copy-start.1
  357.3 6.7 %fusion.4 = f32[4,16,192,64]{2,3,1,0:T(8,128)S(1)} fusion(bf16[4,192,16,64]{1,3,2,0:T(8,128)(2,1)} %bitcast.40, f32[4,16,192,192]{2,3,1,0:T(8,128)} %get-tuple-element.32, f32[4,16,192]{2,1,0:T(8,128)S(1)} %get-tuple-element.31), kind=kOutput, calls=%fused_computation.7 | convolution fusion | flops 306708480 | bytes 14204928 | tf_op jit(solution)/shard_map/cond/branch_1_fun/mhqk,mkhe->mqhe/dot_general | solution.py:29
  364.0 0.0 copy-done.1
  364.0 1.4 fusion.6
  365.4 2.4 copy.29
  367.7 0.0 copy-start.3
  367.8 3.0 fusion.15
  370.8 0.0 copy-done.3
  370.8 0.3 maximum_bitcast_fusion
  371.1 4.9 %copy.26 = bf16[1,4,192,2,1024]{4,3,2,1,0:T(2,128)(2,1)} copy(bf16[1,4,192,2,1024]{4,2,1,3,0:T(8,128)(2,1)S(1)} %maximum_bitcast_fusion) | data formatting | bytes 6291456 | tf_op jit(solution)/shard_map/broadcast_in_dim | solution.py:55
  (1 shorter events, 0.0 us)
Async XLA Ops:
  6.5 78.0 %copy-start.4 = (f32[1,4096]{1,0:T(1,128)S(1)}, f32[1,4096]{1,0:T(1,128)}, u32[]{:S(2)}) copy-start(f32[1,4096]{1,0:T(1,128)} %param.7) | copy-start | bytes 49156
  6.5 73.7 %all-gather.3.cloned.1.call-start = ((), (), s32[]{:S(2)}) async-start(), calls=%async_computation | async-start | bytes 7864320 | tf_op jit(solution)/shard_map/all_gather | solution.py:35
  7.3 213.4 %all-gather.5.cloned.1.call-start = ((), (), s32[]{:S(2)}) async-start(), calls=%async_computation.1 | async-start | bytes 17301504 | tf_op jit(solution)/shard_map/all_gather | solution.py:42
  80.3 4.6 %copy-start = (bf16[1,4,192,4096]{3,2,1,0:T(8,128)(2,1)S(1)}, bf16[1,4,192,4096]{3,2,1,0:T(8,128)(2,1)}, u32[]{:S(2)}) copy-start(bf16[1,4,192,4096]{3,2,1,0:T(8,128)(2,1)} %all-gather.3.cloned.1.call-done) | copy-start | bytes 18874372
  220.7 12.1 %copy-start.2 = (bf16[1,4,192,4096]{3,2,1,0:T(8,128)(2,1)S(1)}, bf16[1,4,192,4096]{3,2,1,0:T(8,128)(2,1)}, u32[]{:S(2)}) copy-start(bf16[1,4,192,4096]{3,2,1,0:T(8,128)(2,1)} %fusion.13) | copy-start | bytes 18874372
  254.6 72.5 %collective-permute-start = (bf16[4,192,2,1024]{3,1,2,0:T(8,128)(2,1)}, bf16[4,192,2,1024]{3,1,2,0:T(8,128)(2,1)}, u32[]{:S(2)}, u32[]{:S(2)}) collective-permute-start(bf16[4,192,2,1024]{3,1,2,0:T(8,128)(2,1)} %copy.20), channel_id=1, source_target_pairs={{0,128},{1,129},{2,130},{3,131},{4,132},{5,133},{6,134},{7,135},{8... | collective-permute-start | bytes 9437192 | tf_op jit(solution)/shard_map/ppermute | solution.py:12
  261.4 65.7 %copy-start.5 = (s32[4,1]{0,1:T(1,128)S(1)}, s32[4,1]{0,1:T(1,128)}, u32[]{:S(2)}) copy-start(s32[4,1]{0,1:T(1,128)} %param.9) | copy-start | bytes 52
  344.2 1.6 slice-start
  357.3 6.7 %copy-start.1 = (bf16[4,192,2,1024]{1,3,0,2:T(8,128)(2,1)S(1)}, bf16[4,192,2,1024]{1,3,0,2:T(8,128)(2,1)}, u32[]{:S(2)}) copy-start(bf16[4,192,2,1024]{1,3,0,2:T(8,128)(2,1)} %copy.21) | copy-start | bytes 9437188 | tf_op jit(solution)/shard_map/cond
  367.7 3.1 copy-start.3
Sparse Core Ops, SparseCore 0:
  9.2 71.0 all-gather.2
  83.1 137.5 all-gather.4
where the time goes:
time: 383 us
  waiting for transfers between devices  268 us (70%)
  local copies, waits for them, and re-layouts  52.9 us (14%)
  matrix products  32.6 us (9%)
  other arithmetic  14.4 us (4%)
  between operations  13.5 us (4%)
    all_gather x1, waiting for transfers between devices, per_device(): full = lax.all_gather(weights, 'fsdp', axis=1, tiled=True)[0]  130 us
    all_gather x1, waiting for transfers between devices, per_device(): whole = lax.all_gather(inputs, 'seq', axis=3, tiled=True)[0]  72.3 us
    ppermute x1, waiting for transfers between devices, passed_along(): return lax.ppermute(x, axis, pairs)  63.8 us
    dot_general x1, matrix products, per_device(): jnp.dot(rows, full.reshape(width, 2 * local_width), preferred_element_typ...  14.5 us
    unnamed x12, local copies, waits for them, and re-layouts  14.3 us
    another operation x2, local copies, waits for them, and re-layouts  12.7 us
    sub x1, matrix products, attend(): probs = jax.nn.softmax(scores, axis=-1).astype(jnp.bfloat16)  11.5 us
  transfers between devices with their start and end apart: 3, of which 3 were waited for; matrix products, arithmetic and copies ran while one was open for 4% of the time, Pallas kernels for 0%

commit v1 on v0

v1 whole, which is shorter than its diff:
```python
import functools

import jax
import jax.numpy as jnp
import numpy as np
from jax import lax
from jax.experimental import pallas as pl
from jax.experimental.pallas import tpu as pltpu
from jax.sharding import PartitionSpec as P

HD = 64
AXES = ("section", "fsdp", "seq")
ROWS = 128
BIG = 56 * 1024 * 1024


def pairs_of(rule):
    pairs = []
    for s in range(2):
        for z in range(8):
            for y in range(2):
                for c in range(2):
                    for x in range(4):
                        to = rule(s, z, y, c, x)
                        if to is not None:
                            number = lambda s, z, y, c, x: s * 128 + z % 8 * 16 + y * 8 + c * 4 + x % 4
                            pairs.append((number(s, z, y, c, x), number(*to)))
    return pairs


Z_UP = pairs_of(lambda s, z, y, c, x: (s, z + 1, y, c, x))
Z_DOWN = pairs_of(lambda s, z, y, c, x: (s, z - 1, y, c, x))
Y_OTHER = pairs_of(lambda s, z, y, c, x: (s, z, 1 - y, c, x))
CORE_OTHER = pairs_of(lambda s, z, y, c, x: (s, z, y, 1 - c, x))
X_RING = pairs_of(lambda s, z, y, c, x: (s, z, y, c, x + 1 - 2 * c))
TO_ENC = pairs_of(lambda s, z, y, c, x: (0, z, y, c, x) if s == 1 else None)
TO_DEC = pairs_of(lambda s, z, y, c, x: (1, z, y, c, x) if s == 0 else None)


def sent(x, pairs):
    return lax.ppermute(x, AXES, pairs)


def after(x, *others):
    return lax.optimization_barrier((x, *others))[0]


def rows(*parts):
    return jnp.concatenate(parts, axis=0)


LAST = [(0, 6), (0, 3), (0, 4)]
FIRST = [(1, 0), (1, 7), (1, 1), (1, 6), (1, 2)]
SECOND = [(1, 5), (1, 3), (0, 0), (0, 7), (0, 1)]
THIRD = [(1, 4), (0, 2), (0, 5)]
PLACE = np.zeros((2, 2, 8), np.int32)
_at = 0
for _bundle in (LAST, FIRST, SECOND, THIRD):
    for _own in (1, 0):
        for _same, _far in _bundle:
            PLACE[_same, _own, _far] = _at
            _at += 1


def norm_kernel(source_ref, place_ref, gain_ref, x0, x1, x2, x3, out_ref):
    slices = (x0, x1, x2, x3)
    total = 0.0
    for ref in slices:
        v = ref[...].astype(jnp.float32)
        total = total + jnp.sum(v * v, axis=-1, keepdims=True)
    scale = lax.rsqrt(total / 4096 + 1e-06)
    for i, ref in enumerate(slices):
        gain = gain_ref[:, pl.ds(pl.multiple_of(source_ref[i] * 1024, 1024), 1024)]
        normed = (ref[...].astype(jnp.float32) * scale * gain).astype(jnp.bfloat16)
        for b in range(8):
            at = pl.multiple_of(place_ref[i * 8 + b] * ROWS, ROWS)
            out_ref[:, pl.ds(at, ROWS)] = normed[:, b * ROWS:(b + 1) * ROWS]


def norm(source, place, gains, slices):
    tokens = slices[0].shape[0]
    step = 96
    return pl.pallas_call(
        norm_kernel,
        grid_spec=pltpu.PrefetchScalarGridSpec(
            num_scalar_prefetch=2,
            grid=(tokens // step,),
            in_specs=[pl.BlockSpec((1, 4096), lambda i, *_: (0, 0))]
            + [pl.BlockSpec((step, 1024), lambda i, *_: (i, 0))] * 4,
            out_specs=pl.BlockSpec((step, 4096), lambda i, *_: (i, 0)),
        ),
        out_shape=jax.ShapeDtypeStruct((tokens, 4096), jnp.bfloat16),
        compiler_params=pltpu.CompilerParams(vmem_limit_bytes=BIG),
        cost_estimate=pl.CostEstimate(flops=tokens * 4096 * 6, bytes_accessed=tokens * 4096 * 4, transcendentals=tokens),
    )(source, place, gains, *slices)


def matmul_kernel(depths, start, n_in, x_ref, *refs):
    out_ref = refs[-1]
    total = refs[n_in - 1][...] if n_in > len(depths) else None
    at = start
    for ref, depth in zip(refs, depths):
        part = jnp.dot(x_ref[:, at:at + depth], ref[...], preferred_element_type=jnp.float32)
        total = part if total is None else total + part
        at += depth
    out_ref[...] = total.astype(out_ref.dtype)


def matmul(x, x_block, start, parts, base, dtype, width, column, tile=256):
    tokens = x.shape[0]
    depths = [p.shape[0] for p in parts]
    first = column // tile
    in_specs = [pl.BlockSpec((tokens, x_block), lambda j: (0, 0))]
    in_specs += [pl.BlockSpec((d, tile), lambda j: (0, first + j)) for d in depths]
    args = [x, *parts]
    if base is not None:
        in_specs.append(pl.BlockSpec((tokens, tile), lambda j: (0, first + j)))
        args.append(base)
    return pl.pallas_call(
        functools.partial(matmul_kernel, depths, start, len(args) - 1),
        grid=(width // tile,),
        in_specs=in_specs,
        out_specs=pl.BlockSpec((tokens, tile), lambda j: (0, j)),
        out_shape=jax.ShapeDtypeStruct((tokens, width), dtype),
        compiler_params=pltpu.CompilerParams(vmem_limit_bytes=BIG),
        cost_estimate=pl.CostEstimate(
            flops=2 * tokens * sum(depths) * width,
            bytes_accessed=2 * (tokens + width) * sum(depths) + 6 * tokens * width,
            transcendentals=0,
        ),
    )(*args)


def attend_kernel(index, limit_ref, q_ref, k_ref, v_ref, out_ref):
    tok, width = q_ref.shape
    valid = lax.broadcasted_iota(jnp.int32, (tok, tok), 1) < limit_ref[index]
    low = lax.broadcasted_iota(jnp.int32, (tok, 2 * HD), 1) < HD
    for pair in range(width // (2 * HD)):
        cols = slice(pair * 2 * HD, (pair + 1) * 2 * HD)
        q, k, v = q_ref[:, cols], k_ref[:, cols], v_ref[:, cols]
        halves = []
        for mine in (low, ~low):
            scores = lax.dot_general(
                jnp.where(mine, q, jnp.zeros_like(q)), k, (((1,), (1,)), ((), ())), preferred_element_type=jnp.float32
            ) * 0.125
            scores = jnp.where(valid, scores, jnp.float32(-1e30))
            top = jnp.max(scores, axis=-1, keepdims=True)
            e = jnp.exp(scores - top)
            probs = (e * (1.0 / jnp.sum(e, axis=-1, keepdims=True))).astype(jnp.bfloat16)
            halves.append(jnp.dot(probs, v, preferred_element_type=jnp.float32))
        out_ref[:, cols] = jnp.where(low, halves[0], halves[1]).astype(out_ref.dtype)


def attend(index, limit, q, k, v):
    tok, width = q.shape
    return pl.pallas_call(
        functools.partial(attend_kernel, index),
        grid_spec=pltpu.PrefetchScalarGridSpec(
            num_scalar_prefetch=1,
            grid=(1,),
            in_specs=[
                pl.BlockSpec((tok, width), lambda i, *_: (0, 0)),
                pl.BlockSpec((tok, width), lambda i, *_: (index, 0)),
                pl.BlockSpec((tok, width), lambda i, *_: (index, 0)),
            ],
            out_specs=pl.BlockSpec((tok, width), lambda i, *_: (0, 0)),
        ),
        out_shape=jax.ShapeDtypeStruct((tok, width), jnp.bfloat16),
        compiler_params=pltpu.CompilerParams(vmem_limit_bytes=BIG),
        cost_estimate=pl.CostEstimate(
            flops=4 * tok * tok * width * 2, bytes_accessed=8 * tok * width, transcendentals=tok * tok * width // HD
        ),
    )(limit, q, k, v)


def per_device(inputs, gains, weights, lengths):
    _, batch, tok, wide = inputs.shape
    fsdp, seq = lax.axis_index("fsdp"), lax.axis_index("seq")
    z, y, core = fsdp // 4, fsdp // 2 % 2, fsdp % 2
    is_decoder = lax.axis_index("section") == 1

    steps = np.arange(4, dtype=np.int32)
    source = (seq + (2 * core - 1) * steps) % 4
    block = (source[:, None] * 8 + np.arange(8, dtype=np.int32)[None, :]).reshape(32)
    same = (block // 2 % 2 == y).astype(jnp.int32)
    own = (block % 2 == core).astype(jnp.int32)
    place = jnp.asarray(PLACE).reshape(32)[(same * 2 + own) * 8 + (block // 4 - z) % 8]

    x0 = inputs.reshape(batch * tok, wide)
    w0 = weights.reshape(ROWS, 2 * wide)

    up1, down1 = sent(w0, Z_UP), sent(w0, Z_DOWN)
    other0 = sent(w0, Y_OTHER)
    x1 = sent(x0, X_RING)

    up2, down2 = sent(up1, Z_UP), sent(down1, Z_DOWN)
    other1 = sent(rows(up1, down1), Y_OTHER)
    x2 = sent(x1, X_RING)

    first = rows(w0, up1, down1, up2, down2)
    first_o = sent(first, CORE_OTHER)
    up3, down3 = sent(after(up2, x1, other0), Z_UP), sent(down2, Z_DOWN)
    x3 = sent(x2, X_RING)

    up4 = sent(after(up3, x2, first_o), Z_UP)
    p_down2 = sent(other1[ROWS:], Z_DOWN)
    other3 = sent(up3, Y_OTHER)
    second = rows(up3, down3, other0, other1)
    second_o = sent(second, CORE_OTHER)

    p_up2 = sent(after(other1[:ROWS], up4, x3, second_o), Z_UP)
    p_down3 = sent(p_down2, Z_DOWN)
    other4 = sent(after(up4, other3), Y_OTHER)
    third = rows(up4, p_down2, other3)
    third_o = sent(third, CORE_OTHER)

    normed = norm(source, place, gains, (x0, x1, x2, x3))
    begun = matmul(
        normed, 4096, 6 * ROWS, (first, first_o, second, second_o, third, third_o), None, jnp.float32, 2 * wide, 0
    )

    last = rows(p_up2, p_down3, other4)
    last_o = sent(last, CORE_OTHER)
    front = matmul(normed, 6 * ROWS, 0, (last, last_o), begun, jnp.bfloat16, wide, 0, 512)
    queries = [sent(front[i * tok:(i + 1) * tok], TO_ENC) for i in range(batch)]
    back = matmul(normed, 6 * ROWS, 0, (last, last_o), begun, jnp.bfloat16, wide, wide, 512)

    limit = lengths.reshape(batch)
    context = [sent(attend(i, limit, queries[i], front, back), TO_DEC) for i in range(batch)]
    context = rows(*context).astype(jnp.float32)
    attended = (jax.nn.sigmoid(back.astype(jnp.float32)) * context).astype(jnp.bfloat16)
    final = jnp.stack([jnp.where(is_decoder, attended, front), back], axis=1)
    return final.reshape(1, batch, tok, 2, wide)


def solution(mesh):
    in_specs = (
        P("section", None, "fsdp", "seq"),
        P("section", None),
        P("section", "fsdp", None, "seq"),
        P(None, "fsdp"),
    )
    out_specs = P("section", None, "fsdp", None, "seq")
    return jax.shard_map(
        per_device, mesh=mesh, in_specs=in_specs, out_specs=out_specs, check_vma=False
    )
```

time: 383 us -> 211 us (0.55)
  waiting for transfers between devices: 268 us -> 82.7 us
  Pallas kernels: 0 us -> 57.9 us
  starting transfers between devices: 1.5 us -> 39.4 us
  local copies, waits for them, and re-layouts: 52.9 us -> 18.3 us
  matrix products: 32.6 us -> 0 us
  between operations: 13.5 us -> 0.43 us
    all_gather x2 -> x0, waiting for transfers between devices: 203 us -> none  [the longest x1 130 us: per_device(): full = lax.all_gather(weights, 'fsdp', axis=1, tiled=True)[0]]
    pallas_call x0 -> x8, Pallas kernels: none -> 57.9 us  [the longest x3 29.2 us: matmul(): pl.pallas_call(functools.partial(matmul_kernel, depths, start, len(args)...]
    ppermute x1 -> x29, starting transfers between devices: 1.46 us -> 39.4 us  [sent(): return lax.ppermute(x, AXES, pairs)]
    dot_general x2 -> x0, matrix products: 21.1 us -> none  [the longest x1 14.5 us: per_device(): jnp.dot(rows, full.reshape(width, 2 * local_width), preferred_element_typ...]
    ppermute x1 -> x29, waiting for transfers between devices: 63.8 us -> 82.7 us  [sent(): return lax.ppermute(x, AXES, pairs)]
    sub x1 -> x0, matrix products: 11.5 us -> none  [attend(): probs = jax.nn.softmax(scores, axis=-1).astype(jnp.bfloat16)]
    slice x4 -> x2, local copies, waits for them, and re-layouts: 11.3 us -> 1.54 us  [the longest x1 1.47 us: per_device(): queries = [sent(front[i * tok:(i + 1) * tok], TO_ENC) for i in range(batch)]]
    another operation x2, local copies, waits for them, and re-layouts: 12.7 us -> 4.85 us  [per_device(): final = jnp.stack([jnp.where(is_decoder, attended, front), back], axis=1)]
  transfers between devices with their start and end apart: 3 -> 29, of which waited for: 3 -> 14; matrix products, arithmetic and copies ran while one was open for 4% -> 5% of each run, Pallas kernels for 0% -> 25%
where the time goes in v1:
time: 211 us; the launch traced here: 210 us
  waiting for transfers between devices  82.7 us (39%)
  Pallas kernels  57.9 us (27%)
  starting transfers between devices  39.4 us (19%)
  local copies, waits for them, and re-layouts  18.3 us (9%)
  other arithmetic  11.2 us (5%)
    ppermute x29, waiting for transfers between devices, sent(): return lax.ppermute(x, AXES, pairs)  82.7 us
    ppermute x29, starting transfers between devices, sent(): return lax.ppermute(x, AXES, pairs)  39.4 us
    pallas_call x3, Pallas kernels, matmul(): pl.pallas_call(functools.partial(matmul_kernel, depths, start, len(args)...  29.2 us
    pallas_call x4, Pallas kernels, attend(): pl.pallas_call(functools.partial(attend_kernel, index), grid_spec=pltpu.P...  18.2 us
    pallas_call x1, Pallas kernels, norm(): pl.pallas_call(norm_kernel, grid_spec=pltpu.PrefetchScalarGridSpec(num_sc...  10.5 us
    unnamed x44, local copies, waits for them, and re-layouts  8.46 us
    another operation x1, other arithmetic, per_device(): final = jnp.stack([jnp.where(is_decoder, attended, front), back], axis=1)  8.03 us
    another operation x2, local copies, waits for them, and re-layouts, per_device(): final = jnp.stack([jnp.where(is_decoder, attended, front), back], axis=1)  4.85 us
  transfers between devices with their start and end apart: 29, of which 14 were waited for; matrix products, arithmetic and copies ran while one was open for 5% of the time, Pallas kernels for 25%

profile of v1, /device:TPU:8, one launch (start us, length us, event | category | flops | bytes accessed | tf_op | source)
XLA Modules:
  0.0 209.9 jit_solution(14379748828110380502)
XLA Ops:
  0.0 1.5 collective-permute-start
  1.5 1.2 copy.12
  2.7 2.0 collective-permute-start.3
  4.6 4.0 %collective-permute-start.4 = (bf16[128,2048]{1,0:T(8,128)(2,1)S(1)}, bf16[128,2048]{1,0:T(8,128)(2,1)S(1)}, u32[]{:S(2)}, u32[]{:S(2)}) collective-permute-start(bf16[128,2048]{1,0:T(8,128)(2,1)S(1)} %bitcast.12), channel_id=1, source_target_pairs={{0,112},{1,113},{2,114},{3,115},{4,116},{5,117},{6,118},{7,119},{8... | collective-permute-start | bytes 1572872 | tf_op jit(solution)/shard_map/ppermute | solution.py:41
  8.7 2.3 %collective-permute-start.7 = (bf16[128,2048]{1,0:T(8,128)(2,1)S(1)}, bf16[128,2048]{1,0:T(8,128)(2,1)S(1)}, u32[]{:S(2)}, u32[]{:S(2)}) collective-permute-start(bf16[128,2048]{1,0:T(8,128)(2,1)S(1)} %bitcast.13), channel_id=1, source_target_pairs={{0,8},{1,9},{2,10},{3,11},{4,12},{5,13},{6,14},{7,15},{8,0},{9,1},... | collective-permute-start | bytes 1572872 | tf_op jit(solution)/shard_map/ppermute | solution.py:41
  11.0 10.3 %collective-permute-done.3 = bf16[128,2048]{1,0:T(8,128)(2,1)S(1)} collective-permute-done((bf16[128,2048]{1,0:T(8,128)(2,1)S(1)}, bf16[128,2048]{1,0:T(8,128)(2,1)S(1)}, u32[]{:S(2)}, u32[]{:S(2)}) %collective-permute-start.3) | collective-permute-done | bytes 524320 | tf_op jit(solution)/shard_map/ppermute | solution.py:41
  21.3 3.3 %collective-permute-start.9 = (bf16[128,2048]{1,0:T(8,128)(2,1)S(1)}, bf16[128,2048]{1,0:T(8,128)(2,1)S(1)}, u32[]{:S(2)}, u32[]{:S(2)}) collective-permute-start(bf16[128,2048]{1,0:T(8,128)(2,1)S(1)} %collective-permute-done.4), channel_id=1, source_target_pairs={{0,112},{1,113},{2,114},{3,115},{4,116},{5,117},{6,118},{7,119},{8... | collective-permute-start | bytes 1572872 | tf_op jit(solution)/shard_map/ppermute | solution.py:41
  24.7 2.4 %collective-permute-start.5 = (bf16[256,2048]{1,0:T(8,128)(2,1)S(1)}, bf16[256,2048]{1,0:T(8,128)(2,1)S(1)}, u32[]{:S(2)}, u32[]{:S(2)}) collective-permute-start(bf16[256,2048]{1,0:T(8,128)(2,1)S(1)} %pad_maximum_fusion.1), channel_id=1, source_target_pairs={{0,8},{1,9},{2,10},{3,11},{4,12},{5,13},{6,14},{7,15},{8,0},{9,1},... | collective-permute-start | bytes 3145736 | tf_op jit(solution)/shard_map/ppermute | solution.py:41
  27.1 9.4 %collective-permute-done.6 = bf16[128,2048]{1,0:T(8,128)(2,1)S(1)} collective-permute-done((bf16[128,2048]{1,0:T(8,128)(2,1)S(1)}, bf16[128,2048]{1,0:T(8,128)(2,1)S(1)}, u32[]{:S(2)}, u32[]{:S(2)}) %collective-permute-start.6) | collective-permute-done | bytes 524320 | tf_op jit(solution)/shard_map/ppermute | solution.py:41
  36.6 3.3 %collective-permute-start.12 = (bf16[128,2048]{1,0:T(8,128)(2,1)S(1)}, bf16[128,2048]{1,0:T(8,128)(2,1)S(1)}, u32[]{:S(2)}, u32[]{:S(2)}) collective-permute-start(bf16[128,2048]{1,0:T(8,128)(2,1)S(1)} %collective-permute-done.9), channel_id=1, source_target_pairs={{0,112},{1,113},{2,114},{3,115},{4,116},{5,117},{6,118},{7,119},{8... | collective-permute-start | bytes 1572872 | tf_op jit(solution)/shard_map/ppermute | solution.py:41
  40.2 10.8 %collective-permute-done.8 = bf16[128,2048]{1,0:T(8,128)(2,1)S(1)} collective-permute-done((bf16[128,2048]{1,0:T(8,128)(2,1)S(1)}, bf16[128,2048]{1,0:T(8,128)(2,1)S(1)}, u32[]{:S(2)}, u32[]{:S(2)}) %collective-permute-start.8) | collective-permute-done | bytes 524320 | tf_op jit(solution)/shard_map/ppermute | solution.py:41
  51.4 10.4 %collective-permute-done.1.x2 = bf16[768,1024]{1,0:T(8,128)(2,1)S(1)} collective-permute-done((bf16[768,1024]{1,0:T(8,128)(2,1)S(1)}, bf16[768,1024]{1,0:T(8,128)(2,1)S(1)}, u32[]{:S(2)}, u32[]{:S(2)}) %collective-permute-start.1) | collective-permute-done | bytes 1572896 | tf_op jit(solution)/shard_map/ppermute | solution.py:41
  62.0 2.0 collective-permute-start.11
  64.0 2.3 %collective-permute-start.17 = (bf16[128,2048]{1,0:T(8,128)(2,1)S(1)}, bf16[128,2048]{1,0:T(8,128)(2,1)S(1)}, u32[]{:S(2)}, u32[]{:S(2)}) collective-permute-start(bf16[128,2048]{1,0:T(8,128)(2,1)S(1)} %collective-permute-done.8), channel_id=1, source_target_pairs={{0,8},{1,9},{2,10},{3,11},{4,12},{5,13},{6,14},{7,15},{8,0},{9,1},... | collective-permute-start | bytes 1572872 | tf_op jit(solution)/shard_map/ppermute | solution.py:41
  66.3 8.8 %collective-permute-done.15 = bf16[128,2048]{1,0:T(8,128)(2,1)S(1)} collective-permute-done((bf16[128,2048]{1,0:T(8,128)(2,1)S(1)}, bf16[128,2048]{1,0:T(8,128)(2,1)S(1)}, u32[]{:S(2)}, u32[]{:S(2)}) %collective-permute-start.15) | collective-permute-done | bytes 524320 | tf_op jit(solution)/shard_map/ppermute | solution.py:41
  75.1 1.5 collective-permute-start.16
  77.4 6.0 %collective-permute-done.2.x3 = bf16[768,1024]{1,0:T(8,128)(2,1)S(1)} collective-permute-done((bf16[768,1024]{1,0:T(8,128)(2,1)S(1)}, bf16[768,1024]{1,0:T(8,128)(2,1)S(1)}, u32[]{:S(2)}, u32[]{:S(2)}) %collective-permute-start.2) | collective-permute-done | bytes 1572896 | tf_op jit(solution)/shard_map/ppermute | solution.py:41
  85.3 2.4 %collective-permute-start.18 = (bf16[128,2048]{1,0:T(8,128)(2,1)S(1)}, bf16[128,2048]{1,0:T(8,128)(2,1)}, u32[]{:S(2)}, u32[]{:S(2)}) collective-permute-start(bf16[128,2048]{1,0:T(8,128)(2,1)S(1)} %collective-permute-done.11), channel_id=1, source_target_pairs={{0,8},{1,9},{2,10},{3,11},{4,12},{5,13},{6,14},{7,15},{8,0},{9,1},... | collective-permute-start | bytes 1572872 | tf_op jit(solution)/shard_map/ppermute | solution.py:41
  87.7 7.2 %collective-permute-done.14 = bf16[128,2048]{1,0:T(8,128)(2,1)} collective-permute-done((bf16[128,2048]{1,0:T(8,128)(2,1)S(1)}, bf16[128,2048]{1,0:T(8,128)(2,1)}, u32[]{:S(2)}, u32[]{:S(2)}) %collective-permute-start.14) | collective-permute-done | bytes 524320 | tf_op jit(solution)/shard_map/ppermute | solution.py:41
  96.0 5.2 %collective-permute-done.18 = bf16[128,2048]{1,0:T(8,128)(2,1)} collective-permute-done((bf16[128,2048]{1,0:T(8,128)(2,1)S(1)}, bf16[128,2048]{1,0:T(8,128)(2,1)}, u32[]{:S(2)}, u32[]{:S(2)}) %collective-permute-start.18) | collective-permute-done | bytes 524320 | tf_op jit(solution)/shard_map/ppermute | solution.py:41
  103.3 1.2 gather_fusion
  104.6 10.5 %shard_map.73.x_ref = bf16[768,4096]{1,0:T(8,128)(2,1)} custom-call(s32[4]{0:T(128)} %get-tuple-element.14.source_ref, s32[32]{0:T(128)} %gather_fusion, f32[1,4096]{1,0:T(1,128)} %gain_ref.1, bf16[768,1024]{1,0:T(8,128)(2,1)} %bitcast.16, bf16[768,1024]{1,0:T(8,128)(2,1)} %copy-done.5, bf16[768,1024]{1,0:T(8,128)(2,1)} %copy-done.6, bf16[768,1024]{1,0:T(8,128)(2,1)} %copy-done.7), custom_call_target="tpu_custom_call" | custom-call | flops 18874368 | bytes 12582912 | tf_op jit(solution)/shard_map/pallas_call | solution.py:83
  115.0 19.1 %shard_map.74.refs_2_ = f32[768,2048]{1,0:T(8,128)} custom-call(bf16[768,4096]{1,0:T(8,128)(2,1)} %shard_map.73.x_ref, bf16[640,2048]{1,0:T(8,128)(2,1)} %copy-done.12, bf16[640,2048]{1,0:T(8,128)(2,1)} %copy-done.14, bf16[640,2048]{1,0:T(8,128)(2,1)} %copy-done.13, bf16[640,2048]{1,0:T(8,128)(2,1)} %copy-done.15, ...), custom_call_target="tpu_custom_call" | custom-call | flops 10468982784 | bytes 28180480 | tf_op jit(solution)/shard_map/pallas_call | solution.py:119
  134.2 1.1 copy-done.4
  135.3 5.0 %shard_map.76.k_ref = bf16[768,1024]{1,0:T(8,128)(2,1)} custom-call(bf16[768,4096]{1,0:T(8,128)(2,1)} %shard_map.73.x_ref, bf16[384,2048]{1,0:T(8,128)(2,1)} %copy-done.3, bf16[384,2048]{1,0:T(8,128)(2,1)} %copy-done.4, f32[768,2048]{1,0:T(8,128)} %shard_map.74.refs_2_), custom_call_target="tpu_custom_call" | custom-call | flops 1207959552 | bytes 7471104 | tf_op jit(solution)/shard_map/pallas_call | solution.py:119
  140.3 1.5 fusion.7
  141.8 2.4 %collective-permute-start.21 = (bf16[192,1024]{1,0:T(8,128)(2,1)S(1)}, bf16[192,1024]{1,0:T(8,128)(2,1)S(1)}, u32[]{:S(2)}, u32[]{:S(2)}) collective-permute-start(bf16[192,1024]{1,0:T(8,128)(2,1)S(1)} %get-tuple-element.15), channel_id=1, source_target_pairs={{128,0},{129,1},{130,2},{131,3},{132,4},{133,5},{134,6},{135,7},{1... | collective-permute-start | bytes 1179656 | tf_op jit(solution)/shard_map/ppermute | solution.py:41
  144.2 1.3 collective-permute-start.27
  145.5 1.3 collective-permute-start.25
  146.9 1.3 collective-permute-start.23
  148.2 5.1 %shard_map.75.v_ref = bf16[768,1024]{1,0:T(8,128)(2,1)} custom-call(bf16[768,4096]{1,0:T(8,128)(2,1)} %shard_map.73.x_ref, bf16[384,2048]{1,0:T(8,128)(2,1)} %copy-done.3, bf16[384,2048]{1,0:T(8,128)(2,1)} %copy-done.4, f32[768,2048]{1,0:T(8,128)} %shard_map.74.refs_2_), custom_call_target="tpu_custom_call" | custom-call | flops 1207959552 | bytes 7471104 | tf_op jit(solution)/shard_map/pallas_call | solution.py:119
  154.4 4.5 %shard_map.77 = bf16[192,1024]{1,0:T(8,128)(2,1)} custom-call(s32[4]{0:T(128)} %bitcast.18, bf16[192,1024]{1,0:T(8,128)(2,1)} %copy-done.11, bf16[768,1024]{1,0:T(8,128)(2,1)} %shard_map.76.k_ref, bf16[768,1024]{1,0:T(8,128)(2,1)} %shard_map.75.v_ref), custom_call_target="tpu_custom_call" | custom-call | flops 301989888 | bytes 1572864 | tf_op jit(solution)/shard_map/pallas_call | solution.py:156
  158.9 1.3 collective-permute-start.22
  160.2 1.8 collective-permute-done.27.q_ref
  162.8 4.6 %shard_map.80 = bf16[192,1024]{1,0:T(8,128)(2,1)} custom-call(s32[4]{0:T(128)} %bitcast.19, bf16[192,1024]{1,0:T(8,128)(2,1)} %copy-done.10, bf16[768,1024]{1,0:T(8,128)(2,1)} %shard_map.76.k_ref, bf16[768,1024]{1,0:T(8,128)(2,1)} %shard_map.75.v_ref), custom_call_target="tpu_custom_call" | custom-call | flops 301989888 | bytes 1572864 | tf_op jit(solution)/shard_map/pallas_call | solution.py:156
  167.4 1.5 collective-permute-start.28
  168.9 1.6 collective-permute-done.25.q_ref
  171.2 4.6 %shard_map.79 = bf16[192,1024]{1,0:T(8,128)(2,1)} custom-call(s32[4]{0:T(128)} %bitcast.20, bf16[192,1024]{1,0:T(8,128)(2,1)} %copy-done.9, bf16[768,1024]{1,0:T(8,128)(2,1)} %shard_map.76.k_ref, bf16[768,1024]{1,0:T(8,128)(2,1)} %shard_map.75.v_ref), custom_call_target="tpu_custom_call" | custom-call | flops 301989888 | bytes 1572864 | tf_op jit(solution)/shard_map/pallas_call | solution.py:156
  175.8 1.4 collective-permute-start.26
  177.2 1.1 collective-permute-done.23.q_ref
  179.1 4.5 %shard_map.78 = bf16[192,1024]{1,0:T(8,128)(2,1)} custom-call(s32[4]{0:T(128)} %bitcast.21, bf16[192,1024]{1,0:T(8,128)(2,1)} %copy-done.8, bf16[768,1024]{1,0:T(8,128)(2,1)} %shard_map.76.k_ref, bf16[768,1024]{1,0:T(8,128)(2,1)} %shard_map.75.v_ref), custom_call_target="tpu_custom_call" | custom-call | flops 301989888 | bytes 1572864 | tf_op jit(solution)/shard_map/pallas_call | solution.py:156
  183.6 1.4 collective-permute-start.24
  185.1 2.4 %copy.11 = bf16[1,4,192,1,1024]{4,3,2,1,0:T(2,128)(2,1)S(1)} copy(bf16[1,4,192,1,1024]{4,2,1,3,0:T(8,128)(2,1)S(1)} %bitcast.9) | data formatting | bytes 3145728 | tf_op jit(solution)/shard_map/stack | solution.py:232
  187.5 1.6 collective-permute-done.26
  189.1 8.0 %collective-permute-done.24 = bf16[192,1024]{1,0:T(8,128)(2,1)} collective-permute-done((bf16[192,1024]{1,0:T(8,128)(2,1)}, bf16[192,1024]{1,0:T(8,128)(2,1)}, u32[]{:S(2)}, u32[]{:S(2)}) %collective-permute-start.24) | collective-permute-done | bytes 393248 | tf_op jit(solution)/shard_map/ppermute | solution.py:41
  197.1 2.2 %fusion = bf16[768,1024]{1,0:T(8,128)(2,1)S(1)} fusion(bf16[768,1024]{1,0:T(8,128)(2,1)S(1)} %copy-done.1, bf16[768,1024]{1,0:T(8,128)(2,1)S(1)} %copy-done.2, bf16[192,1024]{1,0:T(8,128)(2,1)} %collective-permute-done.28, bf16[192,1024]{1,0:T(8,128)(2,1)} %collective-permute-done.26, bf16[192,1024]{1,0:T(8,128)(2,1)} %collective-permute-done.24, ...), kind=kLoop, calls=%fused_computation.3 | loop fusion | flops 11796480 | bytes 6291457 | tf_op jit(solution)/shard_map/jit(_where)/select_n | solution.py:232
  199.4 2.4 %copy.10 = bf16[1,4,192,1,1024]{4,3,2,1,0:T(2,128)(2,1)S(1)} copy(bf16[1,4,192,1,1024]{4,2,1,3,0:T(8,128)(2,1)S(1)} %bitcast.10) | data formatting | bytes 3145728 | tf_op jit(solution)/shard_map/stack | solution.py:232
  201.8 8.0 %pad_maximum_fusion = bf16[1,4,192,2,1024]{4,3,2,1,0:T(2,128)(2,1)} fusion(bf16[1,4,192,1,1024]{4,3,2,1,0:T(2,128)(2,1)S(1)} %copy.11, bf16[1,4,192,1,1024]{4,3,2,1,0:T(2,128)(2,1)S(1)} %copy.10), kind=kLoop, calls=%fused_computation.1 | loop fusion | flops 6291456 | bytes 6291456 | tf_op jit(solution)/shard_map/stack | solution.py:232
  (79 shorter events, 10.2 us)
Async XLA Ops:
  0.0 36.5 %collective-permute-start = (bf16[768,1024]{1,0:T(8,128)(2,1)}, bf16[768,1024]{1,0:T(8,128)(2,1)S(1)}, u32[]{:S(2)}, u32[]{:S(2)}) collective-permute-start(bf16[768,1024]{1,0:T(8,128)(2,1)} %bitcast.15), channel_id=1, source_target_pairs={{0,1},{1,2},{2,3},{3,0},{4,7},{5,4},{6,5},{7,6},{8,9},{9,10},{10,1... | collective-permute-start | bytes 4718600 | tf_op jit(solution)/shard_map/ppermute | solution.py:41
  2.7 18.6 %collective-permute-start.3 = (bf16[128,2048]{1,0:T(8,128)(2,1)S(1)}, bf16[128,2048]{1,0:T(8,128)(2,1)S(1)}, u32[]{:S(2)}, u32[]{:S(2)}) collective-permute-start(bf16[128,2048]{1,0:T(8,128)(2,1)S(1)} %bitcast.11), channel_id=1, source_target_pairs={{0,16},{1,17},{2,18},{3,19},{4,20},{5,21},{6,22},{7,23},{8,24},{9,... | collective-permute-start | bytes 1572872 | tf_op jit(solution)/shard_map/ppermute | solution.py:41
  4.6 16.6 %collective-permute-start.4 = (bf16[128,2048]{1,0:T(8,128)(2,1)S(1)}, bf16[128,2048]{1,0:T(8,128)(2,1)S(1)}, u32[]{:S(2)}, u32[]{:S(2)}) collective-permute-start(bf16[128,2048]{1,0:T(8,128)(2,1)S(1)} %bitcast.12), channel_id=1, source_target_pairs={{0,112},{1,113},{2,114},{3,115},{4,116},{5,117},{6,118},{7,119},{8... | collective-permute-start | bytes 1572872 | tf_op jit(solution)/shard_map/ppermute | solution.py:41
  8.7 18.5 %collective-permute-start.7 = (bf16[128,2048]{1,0:T(8,128)(2,1)S(1)}, bf16[128,2048]{1,0:T(8,128)(2,1)S(1)}, u32[]{:S(2)}, u32[]{:S(2)}) collective-permute-start(bf16[128,2048]{1,0:T(8,128)(2,1)S(1)} %bitcast.13), channel_id=1, source_target_pairs={{0,8},{1,9},{2,10},{3,11},{4,12},{5,13},{6,14},{7,15},{8,0},{9,1},... | collective-permute-start | bytes 1572872 | tf_op jit(solution)/shard_map/ppermute | solution.py:41
  21.2 15.3 %collective-permute-start.6 = (bf16[128,2048]{1,0:T(8,128)(2,1)S(1)}, bf16[128,2048]{1,0:T(8,128)(2,1)S(1)}, u32[]{:S(2)}, u32[]{:S(2)}) collective-permute-start(bf16[128,2048]{1,0:T(8,128)(2,1)S(1)} %collective-permute-done.3), channel_id=1, source_target_pairs={{0,16},{1,17},{2,18},{3,19},{4,20},{5,21},{6,22},{7,23},{8,24},{9,... | collective-permute-start | bytes 1572872 | tf_op jit(solution)/shard_map/ppermute | solution.py:41
  21.3 15.3 %collective-permute-start.9 = (bf16[128,2048]{1,0:T(8,128)(2,1)S(1)}, bf16[128,2048]{1,0:T(8,128)(2,1)S(1)}, u32[]{:S(2)}, u32[]{:S(2)}) collective-permute-start(bf16[128,2048]{1,0:T(8,128)(2,1)S(1)} %collective-permute-done.4), channel_id=1, source_target_pairs={{0,112},{1,113},{2,114},{3,115},{4,116},{5,117},{6,118},{7,119},{8... | collective-permute-start | bytes 1572872 | tf_op jit(solution)/shard_map/ppermute | solution.py:41
  24.7 26.5 %collective-permute-start.5 = (bf16[256,2048]{1,0:T(8,128)(2,1)S(1)}, bf16[256,2048]{1,0:T(8,128)(2,1)S(1)}, u32[]{:S(2)}, u32[]{:S(2)}) collective-permute-start(bf16[256,2048]{1,0:T(8,128)(2,1)S(1)} %pad_maximum_fusion.1), channel_id=1, source_target_pairs={{0,8},{1,9},{2,10},{3,11},{4,12},{5,13},{6,14},{7,15},{8,0},{9,1},... | collective-permute-start | bytes 3145736 | tf_op jit(solution)/shard_map/ppermute | solution.py:41
  36.5 14.6 %copy-start.5 = (bf16[768,1024]{1,0:T(8,128)(2,1)}, bf16[768,1024]{1,0:T(8,128)(2,1)S(1)}, u32[]{:S(2)}) copy-start(bf16[768,1024]{1,0:T(8,128)(2,1)S(1)} %collective-permute-done.x1) | copy-start | bytes 4718596
  36.5 14.5 %collective-permute-start.8 = (bf16[128,2048]{1,0:T(8,128)(2,1)S(1)}, bf16[128,2048]{1,0:T(8,128)(2,1)S(1)}, u32[]{:S(2)}, u32[]{:S(2)}) collective-permute-start(bf16[128,2048]{1,0:T(8,128)(2,1)S(1)} %collective-permute-done.6), channel_id=1, source_target_pairs={{0,16},{1,17},{2,18},{3,19},{4,20},{5,21},{6,22},{7,23},{8,24},{9,... | collective-permute-start | bytes 1572872 | tf_op jit(solution)/shard_map/ppermute | solution.py:41
  36.6 14.5 %collective-permute-start.12 = (bf16[128,2048]{1,0:T(8,128)(2,1)S(1)}, bf16[128,2048]{1,0:T(8,128)(2,1)S(1)}, u32[]{:S(2)}, u32[]{:S(2)}) collective-permute-start(bf16[128,2048]{1,0:T(8,128)(2,1)S(1)} %collective-permute-done.9), channel_id=1, source_target_pairs={{0,112},{1,113},{2,114},{3,115},{4,116},{5,117},{6,118},{7,119},{8... | collective-permute-start | bytes 1572872 | tf_op jit(solution)/shard_map/ppermute | solution.py:41
  40.0 11.3 %copy-start.12 = (bf16[640,2048]{1,0:T(8,128)(2,1)}, bf16[640,2048]{1,0:T(8,128)(2,1)S(1)}, u32[]{:S(2)}) copy-start(bf16[640,2048]{1,0:T(8,128)(2,1)S(1)} %constant_dynamic-update-slice_fusion.refs_0_) | copy-start | bytes 7864324
  40.0 22.0 %collective-permute-start.10 = (bf16[640,2048]{1,0:T(8,128)(2,1)S(1)}, bf16[640,2048]{1,0:T(8,128)(2,1)S(1)}, u32[]{:S(2)}, u32[]{:S(2)}) collective-permute-start(bf16[640,2048]{1,0:T(8,128)(2,1)S(1)} %constant_dynamic-update-slice_fusion.refs_0_), channel_id=1, source_target_pairs={{0,4},{1,5},{2,6},{3,7},{4,0},{5,1},{6,2},{7,3},{8,12},{9,13},{10,... | collective-permute-start | bytes 7864328 | tf_op jit(solution)/shard_map/ppermute | solution.py:41
  40.1 21.7 %collective-permute-start.1 = (bf16[768,1024]{1,0:T(8,128)(2,1)S(1)}, bf16[768,1024]{1,0:T(8,128)(2,1)S(1)}, u32[]{:S(2)}, u32[]{:S(2)}) collective-permute-start(bf16[768,1024]{1,0:T(8,128)(2,1)S(1)} %collective-permute-done.x1), channel_id=1, source_target_pairs={{0,1},{1,2},{2,3},{3,0},{4,7},{5,4},{6,5},{7,6},{8,9},{9,10},{10,1... | collective-permute-start | bytes 4718600 | tf_op jit(solution)/shard_map/ppermute | solution.py:41
  51.3 36.4 %copy-start.13 = (bf16[640,2048]{1,0:T(8,128)(2,1)}, bf16[640,2048]{1,0:T(8,128)(2,1)S(1)}, u32[]{:S(2)}) copy-start(bf16[640,2048]{1,0:T(8,128)(2,1)S(1)} %constant_dynamic-update-slice_fusion.5.refs_2_) | copy-start | bytes 7864324
  51.3 26.1 %collective-permute-start.13 = (bf16[640,2048]{1,0:T(8,128)(2,1)S(1)}, bf16[640,2048]{1,0:T(8,128)(2,1)S(1)}, u32[]{:S(2)}, u32[]{:S(2)}) collective-permute-start(bf16[640,2048]{1,0:T(8,128)(2,1)S(1)} %constant_dynamic-update-slice_fusion.5.refs_2_), channel_id=1, source_target_pairs={{0,4},{1,5},{2,6},{3,7},{4,0},{5,1},{6,2},{7,3},{8,12},{9,13},{10,... | collective-permute-start | bytes 7864328 | tf_op jit(solution)/shard_map/ppermute | solution.py:41
  61.8 23.4 %copy-start.6 = (bf16[768,1024]{1,0:T(8,128)(2,1)}, bf16[768,1024]{1,0:T(8,128)(2,1)S(1)}, u32[]{:S(2)}) copy-start(bf16[768,1024]{1,0:T(8,128)(2,1)S(1)} %collective-permute-done.1.x2) | copy-start | bytes 4718596
  61.8 21.6 %collective-permute-start.2 = (bf16[768,1024]{1,0:T(8,128)(2,1)S(1)}, bf16[768,1024]{1,0:T(8,128)(2,1)S(1)}, u32[]{:S(2)}, u32[]{:S(2)}) collective-permute-start(bf16[768,1024]{1,0:T(8,128)(2,1)S(1)} %collective-permute-done.1.x2), channel_id=1, source_target_pairs={{0,1},{1,2},{2,3},{3,0},{4,7},{5,4},{6,5},{7,6},{8,9},{9,10},{10,1... | collective-permute-start | bytes 4718600 | tf_op jit(solution)/shard_map/ppermute | solution.py:41
  61.9 13.2 %collective-permute-start.15 = (bf16[128,2048]{1,0:T(8,128)(2,1)S(1)}, bf16[128,2048]{1,0:T(8,128)(2,1)S(1)}, u32[]{:S(2)}, u32[]{:S(2)}) collective-permute-start(bf16[128,2048]{1,0:T(8,128)(2,1)S(1)} %get-tuple-element.19), channel_id=1, source_target_pairs={{0,112},{1,113},{2,114},{3,115},{4,116},{5,117},{6,118},{7,119},{8... | collective-permute-start | bytes 1572872 | tf_op jit(solution)/shard_map/ppermute | solution.py:41
  62.0 25.7 %copy-start.14 = (bf16[640,2048]{1,0:T(8,128)(2,1)}, bf16[640,2048]{1,0:T(8,128)(2,1)S(1)}, u32[]{:S(2)}) copy-start(bf16[640,2048]{1,0:T(8,128)(2,1)S(1)} %collective-permute-done.10.refs_1_) | copy-start | bytes 7864324
  62.0 14.6 %collective-permute-start.11 = (bf16[128,2048]{1,0:T(8,128)(2,1)S(1)}, bf16[128,2048]{1,0:T(8,128)(2,1)S(1)}, u32[]{:S(2)}, u32[]{:S(2)}) collective-permute-start(bf16[128,2048]{1,0:T(8,128)(2,1)S(1)} %collective-permute-done.8), channel_id=1, source_target_pairs={{0,16},{1,17},{2,18},{3,19},{4,20},{5,21},{6,22},{7,23},{8,24},{9,... | collective-permute-start | bytes 1572872 | tf_op jit(solution)/shard_map/ppermute | solution.py:41
  64.0 20.4 %collective-permute-start.17 = (bf16[128,2048]{1,0:T(8,128)(2,1)S(1)}, bf16[128,2048]{1,0:T(8,128)(2,1)S(1)}, u32[]{:S(2)}, u32[]{:S(2)}) collective-permute-start(bf16[128,2048]{1,0:T(8,128)(2,1)S(1)} %collective-permute-done.8), channel_id=1, source_target_pairs={{0,8},{1,9},{2,10},{3,11},{4,12},{5,13},{6,14},{7,15},{8,0},{9,1},... | collective-permute-start | bytes 1572872 | tf_op jit(solution)/shard_map/ppermute | solution.py:41
  75.1 20.9 %collective-permute-start.16 = (bf16[128,2048]{1,0:T(8,128)(2,1)S(1)}, bf16[128,2048]{1,0:T(8,128)(2,1)S(1)}, u32[]{:S(2)}, u32[]{:S(2)}) collective-permute-start(bf16[128,2048]{1,0:T(8,128)(2,1)S(1)} %collective-permute-done.15), channel_id=1, source_target_pairs={{0,112},{1,113},{2,114},{3,115},{4,116},{5,117},{6,118},{7,119},{8... | collective-permute-start | bytes 1572872 | tf_op jit(solution)/shard_map/ppermute | solution.py:41
  77.4 10.3 %copy-start.15 = (bf16[640,2048]{1,0:T(8,128)(2,1)}, bf16[640,2048]{1,0:T(8,128)(2,1)S(1)}, u32[]{:S(2)}) copy-start(bf16[640,2048]{1,0:T(8,128)(2,1)S(1)} %collective-permute-done.13.refs_3_) | copy-start | bytes 7864324
  83.4 1.8 copy-start.7
  83.4 19.9 %copy-start = (s32[32]{0:T(128)S(1)}, s32[32]{0:T(128)}, u32[]{:S(2)}) copy-start(s32[32]{0:T(128)} %constant.128) | copy-start | bytes 388
  83.4 11.4 %collective-permute-start.14 = (bf16[128,2048]{1,0:T(8,128)(2,1)S(1)}, bf16[128,2048]{1,0:T(8,128)(2,1)}, u32[]{:S(2)}, u32[]{:S(2)}) collective-permute-start(bf16[128,2048]{1,0:T(8,128)(2,1)S(1)} %get-tuple-element.11), channel_id=1, source_target_pairs={{0,16},{1,17},{2,18},{3,19},{4,20},{5,21},{6,22},{7,23},{8,24},{9,... | collective-permute-start | bytes 1572872 | tf_op jit(solution)/shard_map/ppermute | solution.py:41
  85.3 29.8 %collective-permute-start.20 = (bf16[384,2048]{1,0:T(8,128)(2,1)}, bf16[384,2048]{1,0:T(8,128)(2,1)}, u32[]{:S(2)}, u32[]{:S(2)}) collective-permute-start(bf16[384,2048]{1,0:T(8,128)(2,1)} %constant_dynamic-update-slice_fusion.12.refs_4_), channel_id=1, source_target_pairs={{0,4},{1,5},{2,6},{3,7},{4,0},{5,1},{6,2},{7,3},{8,12},{9,13},{10,... | collective-permute-start | bytes 4718600 | tf_op jit(solution)/shard_map/ppermute | solution.py:41
  85.3 16.0 %collective-permute-start.18 = (bf16[128,2048]{1,0:T(8,128)(2,1)S(1)}, bf16[128,2048]{1,0:T(8,128)(2,1)}, u32[]{:S(2)}, u32[]{:S(2)}) collective-permute-start(bf16[128,2048]{1,0:T(8,128)(2,1)S(1)} %collective-permute-done.11), channel_id=1, source_target_pairs={{0,8},{1,9},{2,10},{3,11},{4,12},{5,13},{6,14},{7,15},{8,0},{9,1},... | collective-permute-start | bytes 1572872 | tf_op jit(solution)/shard_map/ppermute | solution.py:41
  102.3 12.7 %copy-start.3 = (bf16[384,2048]{1,0:T(8,128)(2,1)}, bf16[384,2048]{1,0:T(8,128)(2,1)S(1)}, u32[]{:S(2)}) copy-start(bf16[384,2048]{1,0:T(8,128)(2,1)S(1)} %constant_dynamic-update-slice_fusion.9.refs_0_) | copy-start | bytes 4718596
  102.3 31.9 %collective-permute-start.19 = (bf16[384,2048]{1,0:T(8,128)(2,1)S(1)}, bf16[384,2048]{1,0:T(8,128)(2,1)S(1)}, u32[]{:S(2)}, u32[]{:S(2)}) collective-permute-start(bf16[384,2048]{1,0:T(8,128)(2,1)S(1)} %constant_dynamic-update-slice_fusion.9.refs_0_), channel_id=1, source_target_pairs={{0,4},{1,5},{2,6},{3,7},{4,0},{5,1},{6,2},{7,3},{8,12},{9,13},{10,... | collective-permute-start | bytes 4718600 | tf_op jit(solution)/shard_map/ppermute | solution.py:41
  134.2 1.1 copy-start.4
  141.8 11.8 %collective-permute-start.21 = (bf16[192,1024]{1,0:T(8,128)(2,1)S(1)}, bf16[192,1024]{1,0:T(8,128)(2,1)S(1)}, u32[]{:S(2)}, u32[]{:S(2)}) collective-permute-start(bf16[192,1024]{1,0:T(8,128)(2,1)S(1)} %get-tuple-element.15), channel_id=1, source_target_pairs={{128,0},{129,1},{130,2},{131,3},{132,4},{133,5},{134,6},{135,7},{1... | collective-permute-start | bytes 1179656 | tf_op jit(solution)/shard_map/ppermute | solution.py:41
  144.2 17.8 %collective-permute-start.27 = (bf16[192,1024]{1,0:T(8,128)(2,1)S(1)}, bf16[192,1024]{1,0:T(8,128)(2,1)S(1)}, u32[]{:S(2)}, u32[]{:S(2)}) collective-permute-start(bf16[192,1024]{1,0:T(8,128)(2,1)S(1)} %get-tuple-element.16), channel_id=1, source_target_pairs={{128,0},{129,1},{130,2},{131,3},{132,4},{133,5},{134,6},{135,7},{1... | collective-permute-start | bytes 1179656 | tf_op jit(solution)/shard_map/ppermute | solution.py:41
  145.5 24.9 %collective-permute-start.25 = (bf16[192,1024]{1,0:T(8,128)(2,1)S(1)}, bf16[192,1024]{1,0:T(8,128)(2,1)S(1)}, u32[]{:S(2)}, u32[]{:S(2)}) collective-permute-start(bf16[192,1024]{1,0:T(8,128)(2,1)S(1)} %get-tuple-element.17), channel_id=1, source_target_pairs={{128,0},{129,1},{130,2},{131,3},{132,4},{133,5},{134,6},{135,7},{1... | collective-permute-start | bytes 1179656 | tf_op jit(solution)/shard_map/ppermute | solution.py:41
  146.9 31.5 %collective-permute-start.23 = (bf16[192,1024]{1,0:T(8,128)(2,1)S(1)}, bf16[192,1024]{1,0:T(8,128)(2,1)S(1)}, u32[]{:S(2)}, u32[]{:S(2)}) collective-permute-start(bf16[192,1024]{1,0:T(8,128)(2,1)S(1)} %get-tuple-element.18), channel_id=1, source_target_pairs={{128,0},{129,1},{130,2},{131,3},{132,4},{133,5},{134,6},{135,7},{1... | collective-permute-start | bytes 1179656 | tf_op jit(solution)/shard_map/ppermute | solution.py:41
  153.6 0.7 copy-start.11
  158.9 28.6 %collective-permute-start.22 = (bf16[192,1024]{1,0:T(8,128)(2,1)}, bf16[192,1024]{1,0:T(8,128)(2,1)S(1)}, u32[]{:S(2)}, u32[]{:S(2)}) collective-permute-start(bf16[192,1024]{1,0:T(8,128)(2,1)} %shard_map.77), channel_id=1, source_target_pairs={{0,128},{1,129},{2,130},{3,131},{4,132},{5,133},{6,134},{7,135},{8... | collective-permute-start | bytes 1179656 | tf_op jit(solution)/shard_map/ppermute | solution.py:41
  162.0 0.7 copy-start.10
  167.4 20.2 %collective-permute-start.28 = (bf16[192,1024]{1,0:T(8,128)(2,1)}, bf16[192,1024]{1,0:T(8,128)(2,1)}, u32[]{:S(2)}, u32[]{:S(2)}) collective-permute-start(bf16[192,1024]{1,0:T(8,128)(2,1)} %shard_map.80), channel_id=1, source_target_pairs={{0,128},{1,129},{2,130},{3,131},{4,132},{5,133},{6,134},{7,135},{8... | collective-permute-start | bytes 1179656 | tf_op jit(solution)/shard_map/ppermute | solution.py:41
  170.5 0.7 copy-start.9
  175.8 9.3 %copy-start.2 = (bf16[768,1024]{1,0:T(8,128)(2,1)S(1)}, bf16[768,1024]{1,0:T(8,128)(2,1)}, u32[]{:S(2)}) copy-start(bf16[768,1024]{1,0:T(8,128)(2,1)} %shard_map.75.v_ref) | copy-start | bytes 4718596
  175.8 13.3 %collective-permute-start.26 = (bf16[192,1024]{1,0:T(8,128)(2,1)}, bf16[192,1024]{1,0:T(8,128)(2,1)}, u32[]{:S(2)}, u32[]{:S(2)}) collective-permute-start(bf16[192,1024]{1,0:T(8,128)(2,1)} %shard_map.79), channel_id=1, source_target_pairs={{0,128},{1,129},{2,130},{3,131},{4,132},{5,133},{6,134},{7,135},{8... | collective-permute-start | bytes 1179656 | tf_op jit(solution)/shard_map/ppermute | solution.py:41
  178.3 0.7 copy-start.8
  183.6 13.5 %copy-start.1 = (bf16[768,1024]{1,0:T(8,128)(2,1)S(1)}, bf16[768,1024]{1,0:T(8,128)(2,1)}, u32[]{:S(2)}) copy-start(bf16[768,1024]{1,0:T(8,128)(2,1)} %shard_map.76.k_ref) | copy-start | bytes 4718596
  183.6 13.5 %collective-permute-start.24 = (bf16[192,1024]{1,0:T(8,128)(2,1)}, bf16[192,1024]{1,0:T(8,128)(2,1)}, u32[]{:S(2)}, u32[]{:S(2)}) collective-permute-start(bf16[192,1024]{1,0:T(8,128)(2,1)} %shard_map.78), channel_id=1, source_target_pairs={{0,128},{1,129},{2,130},{3,131},{4,132},{5,133},{6,134},{7,135},{8... | collective-permute-start | bytes 1179656 | tf_op jit(solution)/shard_map/ppermute | solution.py:41

commit v2 on v1

v2 whole, which is shorter than its diff:
```python
import functools

import jax
import jax.numpy as jnp
import numpy as np
from jax import lax
from jax.experimental import pallas as pl
from jax.experimental.pallas import tpu as pltpu
from jax.sharding import PartitionSpec as P

HD = 64
AXES = ("section", "fsdp", "seq")
ROWS = 128
MIB = 1024 * 1024


def pairs_of(rule):
    pairs = []
    for s in range(2):
        for z in range(8):
            for y in range(2):
                for c in range(2):
                    for x in range(4):
                        to = rule(s, z, y, c, x)
                        if to is not None:
                            number = lambda s, z, y, c, x: s * 128 + z % 8 * 16 + y * 8 + c * 4 + x % 4
                            pairs.append((number(s, z, y, c, x), number(*to)))
    return pairs


Z_UP = pairs_of(lambda s, z, y, c, x: (s, z + 1, y, c, x))
Z_DOWN = pairs_of(lambda s, z, y, c, x: (s, z - 1, y, c, x))
Y_OTHER = pairs_of(lambda s, z, y, c, x: (s, z, 1 - y, c, x))
CORE_OTHER = pairs_of(lambda s, z, y, c, x: (s, z, y, 1 - c, x))
X_RING = pairs_of(lambda s, z, y, c, x: (s, z, y, c, x + 1 - 2 * c))
TO_ENC = pairs_of(lambda s, z, y, c, x: (0, z, y, c, x) if s == 1 else None)
TO_DEC = pairs_of(lambda s, z, y, c, x: (1, z, y, c, x) if s == 0 else None)


def sent(x, pairs):
    return lax.ppermute(x, AXES, pairs)


def after(x, *others):
    return lax.optimization_barrier((x, *others))[0]


def stack_kernel(*refs):
    parts, out, done = refs[:-2], refs[-2], refs[-1]
    copies, at = [], 0
    for k, part in enumerate(parts):
        copies.append(pltpu.make_async_copy(part, out.at[pl.ds(at, part.shape[0])], done.at[k]))
        at += part.shape[0]
    for copy in copies:
        copy.start()
    for copy in copies:
        copy.wait()


def stacked(*parts):
    return pl.pallas_call(
        stack_kernel,
        in_specs=[pl.BlockSpec(memory_space=pl.ANY)] * len(parts),
        out_specs=pl.BlockSpec(memory_space=pl.ANY),
        out_shape=jax.ShapeDtypeStruct((sum(p.shape[0] for p in parts), parts[0].shape[1]), parts[0].dtype),
        scratch_shapes=[pltpu.SemaphoreType.DMA((len(parts),))],
        compiler_params=pltpu.CompilerParams(vmem_limit_bytes=MIB),
        cost_estimate=pl.CostEstimate(flops=0, bytes_accessed=1024, transcendentals=0),
    )(*parts)


LAST = [(0, 6), (0, 3), (0, 4)]
FIRST = [(1, 0), (1, 7), (1, 1), (1, 6), (1, 2)]
SECOND = [(1, 5), (1, 3), (0, 0), (0, 1), (0, 7)]
THIRD = [(1, 4), (0, 2), (0, 5)]
PLACE = np.zeros((2, 2, 8), np.int32)
_at = 0
for _bundle in (LAST, FIRST, SECOND, THIRD):
    for _own in (1, 0):
        for _same, _far in _bundle:
            PLACE[_same, _own, _far] = _at
            _at += 1


def norm_kernel(group, place_ref, gain_ref, x_ref, out_ref):
    places = [pl.multiple_of(place_ref[k] * ROWS, ROWS) for k in range(32)]

    @pl.loop(0, x_ref.shape[0] // group, unroll=True)
    def _(g):
        at = pl.ds(g * group, group)
        values = [x_ref[at, i * 1024:(i + 1) * 1024].astype(jnp.float32) for i in range(4)]
        squares = (values[0] * values[0] + values[1] * values[1]) + (values[2] * values[2] + values[3] * values[3])
        scale = lax.rsqrt(jnp.sum(squares, axis=-1, keepdims=True) / 4096 + 1e-06)
        for i in range(4):
            normed = (values[i] * scale * gain_ref[:, i * 1024:(i + 1) * 1024]).astype(jnp.bfloat16)
            for b in range(8):
                out_ref[at, pl.ds(places[i * 8 + b], ROWS)] = normed[:, b * ROWS:(b + 1) * ROWS]


def norm(place, gains, x):
    tokens, width = x.shape
    step = 64
    return pl.pallas_call(
        functools.partial(norm_kernel, 32),
        grid_spec=pltpu.PrefetchScalarGridSpec(
            num_scalar_prefetch=1,
            grid=(tokens // step,),
            in_specs=[
                pl.BlockSpec((1, width), lambda i, *_: (0, 0)),
                pl.BlockSpec((step, width), lambda i, *_: (i, 0)),
            ],
            out_specs=pl.BlockSpec((step, width), lambda i, *_: (i, 0)),
        ),
        out_shape=jax.ShapeDtypeStruct((tokens, width), jnp.bfloat16),
        compiler_params=pltpu.CompilerParams(vmem_limit_bytes=6 * MIB),
        cost_estimate=pl.CostEstimate(
            flops=tokens * width * 6, bytes_accessed=tokens * width * 4, transcendentals=tokens
        ),
    )(place, gains, x)


def matmul_kernel(start, n_x, n_parts, has_base, tile, pieces, *refs):
    xs, parts = refs[:n_x], refs[n_x:n_x + n_parts]
    outs, held = refs[n_x + n_parts + has_base:-1], refs[-1]
    j = pl.program_id(0)
    depth = 0
    for part in parts:
        held[depth:depth + part.shape[0], :] = part[...]
        depth += part.shape[0]
    row = 0
    for x in xs:
        count = x.shape[0]
        total = jnp.dot(x[:, start:start + depth], held[...], preferred_element_type=jnp.float32)
        if has_base:
            total = total + refs[n_x + n_parts][row:row + count, :]
        for (low, high, left, right), out in zip(pieces, outs):
            begin, end = max(low, row), min(high, row + count)
            if begin < end:

                @pl.when((j >= left // tile) & (j < right // tile))
                def _():
                    out[begin - low:end - low, :] = total[begin - row:end - row].astype(out.dtype)
        row += count


def matmul(xs, x_block, start, parts, base, dtype, width, column, tile, pieces, mib, weight=1):
    tokens = sum(x.shape[0] for x in xs)
    depths = [p.shape[0] for p in parts]
    first = column // tile
    in_specs = [pl.BlockSpec((x.shape[0], x_block), lambda j: (0, 0), pipeline_mode=pl.Buffered(1)) for x in xs]
    in_specs += [pl.BlockSpec((d, tile), lambda j: (0, first + j)) for d in depths]
    args = [*xs, *parts]
    if base is not None:
        in_specs.append(pl.BlockSpec((tokens, tile), lambda j: (0, first + j)))
        args.append(base)

    def placed(left, right):
        return lambda j: (0, jnp.clip(j - left // tile, 0, (right - left) // tile - 1))

    return pl.pallas_call(
        functools.partial(matmul_kernel, start, len(xs), len(parts), base is not None, tile, pieces),
        grid=(width // tile,),
        in_specs=in_specs,
        out_specs=[pl.BlockSpec((high - low, tile), placed(left, right)) for low, high, left, right in pieces],
        out_shape=[jax.ShapeDtypeStruct((high - low, right - left), dtype) for low, high, left, right in pieces],
        scratch_shapes=[pltpu.VMEM((sum(depths), tile), jnp.bfloat16)],
        compiler_params=pltpu.CompilerParams(vmem_limit_bytes=mib * MIB),
        cost_estimate=pl.CostEstimate(
            flops=weight * 2 * tokens * sum(depths) * width,
            bytes_accessed=weight * (2 * (tokens + width) * sum(depths) + 6 * tokens * width),
            transcendentals=0,
        ),
    )(*args)


def attend_kernel(index, limit_ref, q_ref, k_ref, v_ref, out_ref):
    tok, width = q_ref.shape
    valid = lax.broadcasted_iota(jnp.int32, (tok, tok), 1) < limit_ref[index]
    low = lax.broadcasted_iota(jnp.int32, (tok, 2 * HD), 1) < HD
    for pair in range(width // (2 * HD)):
        cols = slice(pair * 2 * HD, (pair + 1) * 2 * HD)
        q, k, v = q_ref[:, cols], k_ref[:, cols], v_ref[:, cols]
        halves = []
        for mine in (low, ~low):
            scores = lax.dot_general(
                jnp.where(mine, q, jnp.zeros_like(q)), k, (((1,), (1,)), ((), ())), preferred_element_type=jnp.float32
            ) * 0.125
            scores = jnp.where(valid, scores, jnp.float32(-1e30))
            top = jnp.max(scores, axis=-1, keepdims=True)
            e = jnp.exp(scores - top)
            probs = (e * (1.0 / jnp.sum(e, axis=-1, keepdims=True))).astype(jnp.bfloat16)
            halves.append(jnp.dot(probs, v, preferred_element_type=jnp.float32))
        out_ref[:, cols] = jnp.where(low, halves[0], halves[1]).astype(out_ref.dtype)


def attend(index, limit, q, k, v):
    tok, width = q.shape
    whole = pl.BlockSpec((tok, width), lambda i, *_: (0, 0))
    return pl.pallas_call(
        functools.partial(attend_kernel, index),
        grid_spec=pltpu.PrefetchScalarGridSpec(
            num_scalar_prefetch=1, grid=(1,), in_specs=[whole, whole, whole], out_specs=whole
        ),
        out_shape=jax.ShapeDtypeStruct((tok, width), jnp.bfloat16),
        compiler_params=pltpu.CompilerParams(vmem_limit_bytes=8 * MIB),
        cost_estimate=pl.CostEstimate(
            flops=4 * tok * tok * width * 2, bytes_accessed=8 * tok * width, transcendentals=tok * tok * width // HD
        ),
    )(limit, q, k, v)


def finish_kernel(decoder_ref, front_ref, back_ref, context_ref, *refs):
    out_ref = refs[-1]

    @pl.when(decoder_ref[0] == 1)
    def _():
        gate = jax.nn.sigmoid(back_ref[...].astype(jnp.float32))
        out_ref[0, 0, :, 0, :] = (gate * context_ref[...].astype(jnp.float32)).astype(out_ref.dtype)

    @pl.when(decoder_ref[0] != 1)
    def _():
        out_ref[0, 0, :, 0, :] = front_ref[...]

    out_ref[0, 0, :, 1, :] = back_ref[...]


def finish(index, column, shape, decoder, front, back, context, begun):
    tok, width = front.shape
    step = tok // 2
    part = pl.BlockSpec((step, width), lambda i, *_: (i, 0))
    args, in_specs, aliases = [front, back, context], [part, part, part], {}
    if begun is not None:
        args.append(begun)
        in_specs.append(pl.BlockSpec(memory_space=pl.ANY))
        aliases = {4: 0}
    return pl.pallas_call(
        finish_kernel,
        grid_spec=pltpu.PrefetchScalarGridSpec(
            num_scalar_prefetch=1,
            grid=(2,),
            in_specs=in_specs,
            out_specs=pl.BlockSpec((1, 1, step, 2, width), lambda i, *_: (0, index, i, 0, column // width)),
        ),
        out_shape=jax.ShapeDtypeStruct(shape, jnp.bfloat16),
        input_output_aliases=aliases,
        compiler_params=pltpu.CompilerParams(vmem_limit_bytes=6 * MIB),
        cost_estimate=pl.CostEstimate(flops=6 * tok * width, bytes_accessed=10 * tok * width, transcendentals=tok * width),
    )(decoder, *args)


def per_device(inputs, gains, weights, lengths):
    _, batch, tok, wide = inputs.shape
    fsdp, seq = lax.axis_index("fsdp"), lax.axis_index("seq")
    z, y, core = fsdp // 4, fsdp // 2 % 2, fsdp % 2
    decoder = lax.axis_index("section").astype(jnp.int32).reshape(1)

    block = np.arange(32, dtype=np.int32)
    same = (block // 2 % 2 == y).astype(jnp.int32)
    own = (block % 2 == core).astype(jnp.int32)
    place = jnp.asarray(PLACE).reshape(32)[(same * 2 + own) * 8 + (block // 4 - z) % 8]

    x = lax.all_gather(inputs, "seq", axis=3, tiled=True)
    tokens = batch * tok
    w0 = weights.reshape(ROWS, 2 * wide)

    up1, down1 = sent(w0, Z_UP), sent(w0, Z_DOWN)
    other0 = sent(w0, Y_OTHER)

    up2, down2 = sent(up1, Z_UP), sent(after(down1, other0), Z_DOWN)
    other_down1 = sent(down1, Y_OTHER)

    up3, down3 = sent(up2, Z_UP), sent(after(down2, other_down1), Z_DOWN)
    other_up1 = sent(up1, Y_OTHER)
    first = stacked(w0, up1, down1, up2, down2)
    first_o = sent(first, CORE_OTHER)

    up4 = sent(up3, Z_UP)
    p_down2 = sent(after(other_down1, down3, other_up1), Z_DOWN)
    other3 = sent(up3, Y_OTHER)
    second = stacked(up3, down3, other0, other_down1, other_up1)
    second_o = sent(second, CORE_OTHER)

    p_up2 = sent(after(other_up1, up4), Z_UP)
    p_down3 = sent(after(p_down2, other3), Z_DOWN)
    other4 = sent(up4, Y_OTHER)
    third = stacked(up4, p_down2, other3)
    third_o = sent(third, CORE_OTHER)

    normed = (norm(place, gains, x.reshape(tokens, 4 * wide)),)
    last = stacked(after(p_up2, *normed), p_down3, other4)
    last_o = sent(last, CORE_OTHER)
    bundles = (last, last_o, first, first_o, second, second_o, third, third_o)
    pieces = [(i * tok, (i + 1) * tok, 0, wide) for i in range(batch - 1)]
    pieces += [(tokens - tok, tokens, 0, wide // 2), (tokens - tok, tokens, wide // 2, wide)]
    front = matmul(normed, 4096, 0, bundles, None, jnp.bfloat16, wide, 0, 256, pieces, 20)
    queries = [sent(piece, TO_ENC) for piece in front]
    back = matmul(normed, 4096, 0, bundles, None, jnp.bfloat16, wide, wide, 256, pieces, 20, 0)

    limit = lengths.reshape(batch)
    shape = (1, batch, tok, 2, wide)
    out, context = None, None
    for (low, _, column, _), query, f, b in zip(pieces, queries, front, back):
        if context is not None:
            query = after(query, context)
        context = attend(low // tok, limit, query, f, b)
        out = finish(low // tok, column, shape, decoder, f, b, sent(context, TO_DEC), out)
    return out


def solution(mesh):
    in_specs = (
        P("section", None, "fsdp", "seq"),
        P("section", None),
        P("section", "fsdp", None, "seq"),
        P(None, "fsdp"),
    )
    out_specs = P("section", None, "fsdp", None, "seq")
    return jax.shard_map(
        per_device, mesh=mesh, in_specs=in_specs, out_specs=out_specs, check_vma=False
    )
```

time: 211 us -> 169 us (0.80)
  waiting for transfers between devices: 82.7 us -> 64 us
  between operations: 0.43 us -> 13.9 us
  other arithmetic: 11.2 us -> 0.02 us
  Pallas kernels: 57.9 us -> 47.4 us
  local copies, waits for them, and re-layouts: 18.3 us -> 7.81 us
  starting transfers between devices: 39.4 us -> 35.3 us
    ppermute x29, waiting for transfers between devices: 82.7 us -> 62.3 us  [sent(): return lax.ppermute(x, AXES, pairs)]
    another operation x1 -> x0, other arithmetic: 8.03 us -> none  [per_device(): final = jnp.stack([jnp.where(is_decoder, attended, front), back], axis=1)]
    pallas_call x4 -> x5, Pallas kernels: 18.2 us -> 12.4 us  [attend(): pl.pallas_call(functools.partial(attend_kernel, index), grid_spec=pltpu.P...]
    another operation x2 -> x0, local copies, waits for them, and re-layouts: 4.85 us -> none  [per_device(): final = jnp.stack([jnp.where(is_decoder, attended, front), back], axis=1)]
    pallas_call x4 -> x12, Pallas kernels: 39.7 us -> 35.1 us  [the longest x2 18.6 us: matmul(): pl.pallas_call(functools.partial(matmul_kernel, start, len(xs), len(parts...]
    ppermute x29, starting transfers between devices: 39.4 us -> 35.3 us  [sent(): return lax.ppermute(x, AXES, pairs)]
    select_n x1 -> x0, other arithmetic: 2.24 us -> none  [per_device(): final = jnp.stack([jnp.where(is_decoder, attended, front), back], axis=1)]
    unnamed x44 -> x55, local copies, waits for them, and re-layouts: 8.46 us -> 7.11 us
  transfers between devices with their start and end apart: 29 -> 30, of which waited for: 14 -> 18; matrix products, arithmetic and copies ran while one was open for 5% -> 1% of each run, Pallas kernels for 25% -> 22%
where the time goes in v2:
time: 169 us
  waiting for transfers between devices  64 us (38%)
  Pallas kernels  47.4 us (28%)
  starting transfers between devices  35.3 us (21%)
  between operations  13.9 us (8%)
  local copies, waits for them, and re-layouts  7.81 us (5%)
    ppermute x29, waiting for transfers between devices, sent(): return lax.ppermute(x, AXES, pairs)  62.3 us
    ppermute x29, starting transfers between devices, sent(): return lax.ppermute(x, AXES, pairs)  35.3 us
    pallas_call x2, Pallas kernels, matmul(): pl.pallas_call(functools.partial(matmul_kernel, start, len(xs), len(parts...  18.6 us
    pallas_call x5, Pallas kernels, attend(): pl.pallas_call(functools.partial(attend_kernel, index), grid_spec=pltpu.P...  12.4 us
    pallas_call x5, Pallas kernels, finish(): pl.pallas_call(finish_kernel, grid_spec=pltpu.PrefetchScalarGridSpec(num_...  8.34 us
    unnamed x55, local copies, waits for them, and re-layouts  7.11 us
    pallas_call x4, Pallas kernels, stacked(): pl.pallas_call(stack_kernel, in_specs=[pl.BlockSpec(memory_space=pl.ANY)]...  4.37 us
    pallas_call x1, Pallas kernels, norm(): pl.pallas_call(functools.partial(norm_kernel, 32), grid_spec=pltpu.Prefet...  3.76 us
  transfers between devices with their start and end apart: 30, of which 18 were waited for; matrix products, arithmetic and copies ran while one was open for 1% of the time, Pallas kernels for 22%

profile of v2, /device:TPU:8, one launch (start us, length us, event | category | flops | bytes accessed | tf_op | source)
XLA Modules:
  0.0 168.5 jit_solution(15429968040627251518)
XLA Ops:
  8.4 2.4 %collective-permute-start.8 = (bf16[128,2048]{1,0:T(8,128)(2,1)S(1)}, bf16[128,2048]{1,0:T(8,128)(2,1)S(1)}, u32[]{:S(2)}, u32[]{:S(2)}) collective-permute-start(bf16[128,2048]{1,0:T(8,128)(2,1)S(1)} %bitcast.7), channel_id=1, source_target_pairs={{0,8},{1,9},{2,10},{3,11},{4,12},{5,13},{6,14},{7,15},{8,0},{9,1},... | collective-permute-start | bytes 1572872 | tf_op jit(solution)/shard_map/ppermute | solution.py:41
  10.8 5.9 %collective-permute-start.6 = (bf16[128,2048]{1,0:T(8,128)(2,1)S(1)}, bf16[128,2048]{1,0:T(8,128)(2,1)S(1)}, u32[]{:S(2)}, u32[]{:S(2)}) collective-permute-start(bf16[128,2048]{1,0:T(8,128)(2,1)S(1)} %bitcast.8), channel_id=1, source_target_pairs={{0,112},{1,113},{2,114},{3,115},{4,116},{5,117},{6,118},{7,119},{8... | collective-permute-start | bytes 1572872 | tf_op jit(solution)/shard_map/ppermute | solution.py:41
  16.7 7.0 %collective-permute-done.8.refs_2_ = bf16[128,2048]{1,0:T(8,128)(2,1)S(1)} collective-permute-done((bf16[128,2048]{1,0:T(8,128)(2,1)S(1)}, bf16[128,2048]{1,0:T(8,128)(2,1)S(1)}, u32[]{:S(2)}, u32[]{:S(2)}) %collective-permute-start.8) | collective-permute-done | bytes 524320 | tf_op jit(solution)/shard_map/ppermute | solution.py:41
  23.7 3.9 %collective-permute-done.6.refs_2_ = bf16[128,2048]{1,0:T(8,128)(2,1)S(1)} collective-permute-done((bf16[128,2048]{1,0:T(8,128)(2,1)S(1)}, bf16[128,2048]{1,0:T(8,128)(2,1)S(1)}, u32[]{:S(2)}, u32[]{:S(2)}) %collective-permute-start.6) | collective-permute-done | bytes 524320 | tf_op jit(solution)/shard_map/ppermute | solution.py:41
  27.6 3.4 %collective-permute-done.refs_1_ = bf16[128,2048]{1,0:T(8,128)(2,1)S(1)} collective-permute-done((bf16[128,2048]{1,0:T(8,128)(2,1)S(1)}, bf16[128,2048]{1,0:T(8,128)(2,1)S(1)}, u32[]{:S(2)}, u32[]{:S(2)}) %collective-permute-start) | collective-permute-done | bytes 524320 | tf_op jit(solution)/shard_map/ppermute | solution.py:41
  31.0 3.2 %collective-permute-start.9 = (bf16[128,2048]{1,0:T(8,128)(2,1)S(1)}, bf16[128,2048]{1,0:T(8,128)(2,1)S(1)}, u32[]{:S(2)}, u32[]{:S(2)}) collective-permute-start(bf16[128,2048]{1,0:T(8,128)(2,1)S(1)} %collective-permute-done.6.refs_2_), channel_id=1, source_target_pairs={{0,112},{1,113},{2,114},{3,115},{4,116},{5,117},{6,118},{7,119},{8... | collective-permute-start | bytes 1572872 | tf_op jit(solution)/shard_map/ppermute | solution.py:41
  34.2 1.2 collective-permute-start.7
  35.4 2.3 %collective-permute-start.1 = (bf16[128,2048]{1,0:T(8,128)(2,1)S(1)}, bf16[128,2048]{1,0:T(8,128)(2,1)S(1)}, u32[]{:S(2)}, u32[]{:S(2)}) collective-permute-start(bf16[128,2048]{1,0:T(8,128)(2,1)S(1)} %collective-permute-done.refs_1_), channel_id=1, source_target_pairs={{0,8},{1,9},{2,10},{3,11},{4,12},{5,13},{6,14},{7,15},{8,0},{9,1},... | collective-permute-start | bytes 1572872 | tf_op jit(solution)/shard_map/ppermute | solution.py:41
  37.7 6.6 %collective-permute-done.2.refs_3_ = bf16[128,2048]{1,0:T(8,128)(2,1)S(1)} collective-permute-done((bf16[128,2048]{1,0:T(8,128)(2,1)S(1)}, bf16[128,2048]{1,0:T(8,128)(2,1)S(1)}, u32[]{:S(2)}, u32[]{:S(2)}) %collective-permute-start.2) | collective-permute-done | bytes 524320 | tf_op jit(solution)/shard_map/ppermute | solution.py:41
  44.4 6.2 %collective-permute-done.7.refs_3_ = bf16[128,2048]{1,0:T(8,128)(2,1)S(1)} collective-permute-done((bf16[128,2048]{1,0:T(8,128)(2,1)S(1)}, bf16[128,2048]{1,0:T(8,128)(2,1)S(1)}, u32[]{:S(2)}, u32[]{:S(2)}) %collective-permute-start.7) | collective-permute-done | bytes 524320 | tf_op jit(solution)/shard_map/ppermute | solution.py:41
  50.6 6.4 %collective-permute-done.3.refs_0_ = bf16[128,2048]{1,0:T(8,128)(2,1)S(1)} collective-permute-done((bf16[128,2048]{1,0:T(8,128)(2,1)S(1)}, bf16[128,2048]{1,0:T(8,128)(2,1)S(1)}, u32[]{:S(2)}, u32[]{:S(2)}) %collective-permute-start.3) | collective-permute-done | bytes 524320 | tf_op jit(solution)/shard_map/ppermute | solution.py:41
  56.9 1.6 collective-permute-done.1.refs_4_
  58.6 1.9 %collective-permute-done.10.refs_1_ = bf16[128,2048]{1,0:T(8,128)(2,1)S(1)} collective-permute-done((bf16[128,2048]{1,0:T(8,128)(2,1)S(1)}, bf16[128,2048]{1,0:T(8,128)(2,1)S(1)}, u32[]{:S(2)}, u32[]{:S(2)}) %collective-permute-start.10) | collective-permute-done | bytes 524320 | tf_op jit(solution)/shard_map/ppermute | solution.py:41
  62.6 1.5 shard_map.85.refs_5_
  64.7 4.1 %collective-permute-done.4.refs_0_ = bf16[128,2048]{1,0:T(8,128)(2,1)} collective-permute-done((bf16[128,2048]{1,0:T(8,128)(2,1)S(1)}, bf16[128,2048]{1,0:T(8,128)(2,1)}, u32[]{:S(2)}, u32[]{:S(2)}) %collective-permute-start.4) | collective-permute-done | bytes 524320 | tf_op jit(solution)/shard_map/ppermute | solution.py:41
  68.8 2.8 %collective-permute-done.12.refs_2_ = bf16[128,2048]{1,0:T(8,128)(2,1)S(1)} collective-permute-done((bf16[128,2048]{1,0:T(8,128)(2,1)S(1)}, bf16[128,2048]{1,0:T(8,128)(2,1)S(1)}, u32[]{:S(2)}, u32[]{:S(2)}) %collective-permute-start.12) | collective-permute-done | bytes 524320 | tf_op jit(solution)/shard_map/ppermute | solution.py:41
  72.4 1.6 collective-permute-start.14
  76.8 1.2 shard_map.86.refs_7_
  80.3 2.8 %copy-done = bf16[1,4,192,4096]{3,2,1,0:T(8,128)(2,1)S(1)} copy-done((bf16[1,4,192,4096]{3,2,1,0:T(8,128)(2,1)S(1)}, bf16[1,4,192,4096]{3,2,1,0:T(8,128)(2,1)}, u32[]{:S(2)}) %copy-start) | copy-done | bytes 6291480
  83.1 3.8 %shard_map.82.refs_0_ = bf16[768,4096]{1,0:T(8,128)(2,1)S(1)} custom-call(s32[32]{0:T(128)S(1)} %gather_fusion, f32[1,4096]{1,0:T(1,128)S(1)} %copy-done.21, bf16[768,4096]{1,0:T(8,128)(2,1)S(1)} %bitcast.6), custom_call_target="tpu_custom_call" | custom-call | flops 18874368 | bytes 12582912 | tf_op jit(solution)/shard_map/pallas_call | solution.py:103
  87.0 1.4 shard_map.83.refs_1_
  88.9 1.4 collective-permute-done.18.refs_8_
  90.3 2.2 %collective-permute-done.15.refs_2_ = bf16[384,2048]{1,0:T(8,128)(2,1)S(1)} collective-permute-done((bf16[384,2048]{1,0:T(8,128)(2,1)S(1)}, bf16[384,2048]{1,0:T(8,128)(2,1)S(1)}, u32[]{:S(2)}, u32[]{:S(2)}) %collective-permute-start.15) | collective-permute-done | bytes 1572896 | tf_op jit(solution)/shard_map/ppermute | solution.py:41
  92.6 9.3 %shard_map.87 = (bf16[192,1024]{1,0:T(8,128)(2,1)S(1)}, bf16[192,1024]{1,0:T(8,128)(2,1)S(1)}, bf16[192,1024]{1,0:T(8,128)(2,1)S(1)}, bf16[192,512]{1,0:T(8,128)(2,1)S(1)}, bf16[192,512]{1,0:T(8,128)(2,1)S(1)}) custom-call(bf16[768,4096]{1,0:T(8,128)(2,1)S(1)} %shard_map.82.refs_0_, bf16[384,2048]{1,0:T(8,128)(2,1)S(1)} %shard_map.83.refs_1_, ...), custom_call_target="tpu_custom_call" | custom-call | flops 6442450944 | bytes 19398656 | tf_op jit(solution)/shard_map/pallas_call | solution.py:160
  101.9 2.6 %collective-permute-start.23 = (bf16[192,1024]{1,0:T(8,128)(2,1)S(1)}, bf16[192,1024]{1,0:T(8,128)(2,1)S(1)}, u32[]{:S(2)}, u32[]{:S(2)}) collective-permute-start(bf16[192,1024]{1,0:T(8,128)(2,1)S(1)} %get-tuple-element.36.k_ref.front_ref), channel_id=1, source_target_pairs={{128,0},{129,1},{130,2},{131,3},{132,4},{133,5},{134,6},{135,7},{1... | collective-permute-start | bytes 1179656 | tf_op jit(solution)/shard_map/ppermute | solution.py:41
  104.5 1.3 collective-permute-start.22
  105.8 1.3 collective-permute-start.21
  107.1 1.3 collective-permute-start.19
  108.5 1.3 collective-permute-start.20
  109.8 9.3 %shard_map.88 = (bf16[192,1024]{1,0:T(8,128)(2,1)S(1)}, bf16[192,1024]{1,0:T(8,128)(2,1)S(1)}, bf16[192,1024]{1,0:T(8,128)(2,1)S(1)}, bf16[192,512]{1,0:T(8,128)(2,1)S(1)}, bf16[192,512]{1,0:T(8,128)(2,1)S(1)}) custom-call(bf16[768,4096]{1,0:T(8,128)(2,1)S(1)} %shard_map.82.refs_0_, bf16[384,2048]{1,0:T(8,128)(2,1)S(1)} %shard_map.83.refs_1_, ...), custom_call_target="tpu_custom_call" | custom-call | tf_op jit(solution)/shard_map/pallas_call | solution.py:160
  119.2 2.4 %shard_map.89 = bf16[192,1024]{1,0:T(8,128)(2,1)S(1)} custom-call(s32[4]{0:T(128)S(1)} %bitcast.11, bf16[192,1024]{1,0:T(8,128)(2,1)S(1)} %collective-permute-done.23.q_ref, bf16[192,1024]{1,0:T(8,128)(2,1)S(1)} %get-tuple-element.36.k_ref.front_ref, bf16[192,1024]{1,0:T(8,128)(2,1)S(1)} %get-tuple-element.37.v_ref.back_ref), custom_call_target="tpu_custom_call" | custom-call | flops 301989888 | bytes 1572864 | tf_op jit(solution)/shard_map/pallas_call | solution.py:199
  121.6 1.3 collective-permute-start.28
  122.9 2.4 %shard_map.90 = bf16[192,1024]{1,0:T(8,128)(2,1)S(1)} custom-call(s32[4]{0:T(128)S(1)} %bitcast.12, bf16[192,1024]{1,0:T(8,128)(2,1)S(1)} %collective-permute-done.22.q_ref, bf16[192,1024]{1,0:T(8,128)(2,1)S(1)} %get-tuple-element.35.k_ref.front_ref, bf16[192,1024]{1,0:T(8,128)(2,1)S(1)} %get-tuple-element.39.v_ref.back_ref), custom_call_target="tpu_custom_call" | custom-call | flops 301989888 | bytes 1572864 | tf_op jit(solution)/shard_map/pallas_call | solution.py:199
  125.4 1.3 collective-permute-start.27
  126.7 4.1 %collective-permute-done.21.q_ref = bf16[192,1024]{1,0:T(8,128)(2,1)S(1)} collective-permute-done((bf16[192,1024]{1,0:T(8,128)(2,1)S(1)}, bf16[192,1024]{1,0:T(8,128)(2,1)S(1)}, u32[]{:S(2)}, u32[]{:S(2)}) %collective-permute-start.21) | collective-permute-done | bytes 393248 | tf_op jit(solution)/shard_map/ppermute | solution.py:41
  130.8 2.4 %shard_map.91 = bf16[192,1024]{1,0:T(8,128)(2,1)S(1)} custom-call(s32[4]{0:T(128)S(1)} %bitcast.13, bf16[192,1024]{1,0:T(8,128)(2,1)S(1)} %collective-permute-done.21.q_ref, bf16[192,1024]{1,0:T(8,128)(2,1)S(1)} %get-tuple-element.34.k_ref.front_ref, bf16[192,1024]{1,0:T(8,128)(2,1)S(1)} %get-tuple-element.41.v_ref.back_ref), custom_call_target="tpu_custom_call" | custom-call | flops 301989888 | bytes 1572864 | tf_op jit(solution)/shard_map/pallas_call | solution.py:199
  133.2 1.3 collective-permute-start.26
  134.5 3.9 %collective-permute-done.20.q_ref = bf16[192,512]{1,0:T(8,128)(2,1)S(1)} collective-permute-done((bf16[192,512]{1,0:T(8,128)(2,1)S(1)}, bf16[192,512]{1,0:T(8,128)(2,1)S(1)}, u32[]{:S(2)}, u32[]{:S(2)}) %collective-permute-start.20) | collective-permute-done | bytes 196640 | tf_op jit(solution)/shard_map/ppermute | solution.py:41
  138.4 2.5 %shard_map.92 = bf16[192,512]{1,0:T(8,128)(2,1)} custom-call(s32[4]{0:T(128)S(1)} %bitcast.14, bf16[192,512]{1,0:T(8,128)(2,1)S(1)} %collective-permute-done.20.q_ref, bf16[192,512]{1,0:T(8,128)(2,1)S(1)} %get-tuple-element.33.k_ref.front_ref, bf16[192,512]{1,0:T(8,128)(2,1)S(1)} %get-tuple-element.43.v_ref.back_ref), custom_call_target="tpu_custom_call" | custom-call | flops 150994944 | bytes 786432 | tf_op jit(solution)/shard_map/pallas_call | solution.py:199
  140.9 1.6 collective-permute-start.25
  142.6 2.5 %shard_map.93 = bf16[192,512]{1,0:T(8,128)(2,1)} custom-call(s32[4]{0:T(128)S(1)} %bitcast.15, bf16[192,512]{1,0:T(8,128)(2,1)S(1)} %collective-permute-done.19.q_ref, bf16[192,512]{1,0:T(8,128)(2,1)S(1)} %get-tuple-element.31.k_ref.front_ref, bf16[192,512]{1,0:T(8,128)(2,1)S(1)} %get-tuple-element.32.v_ref.back_ref), custom_call_target="tpu_custom_call" | custom-call | flops 150994944 | bytes 786432 | tf_op jit(solution)/shard_map/pallas_call | solution.py:199
  145.2 1.3 collective-permute-start.24
  147.7 2.2 %shard_map.95.refs_0_ = bf16[1,4,192,2,1024]{4,3,2,1,0:T(2,128)(2,1)} custom-call(s32[1]{0:T(128)} %bitcast.decoder_ref, bf16[192,1024]{1,0:T(8,128)(2,1)S(1)} %copy-done.6, bf16[192,1024]{1,0:T(8,128)(2,1)S(1)} %copy-done.10, bf16[192,1024]{1,0:T(8,128)(2,1)} %collective-permute-done.27.context_ref, ...), custom_call_target="tpu_custom_call", output_to_operand_aliasing={{}: (4, {})} | custom-call | flops 1179648 | bytes 1966080 | tf_op jit(solution)/shard_map/pallas_call | solution.py:236
  149.9 2.6 %collective-permute-done.26.context_ref = bf16[192,1024]{1,0:T(8,128)(2,1)} collective-permute-done((bf16[192,1024]{1,0:T(8,128)(2,1)S(1)}, bf16[192,1024]{1,0:T(8,128)(2,1)}, u32[]{:S(2)}, u32[]{:S(2)}) %collective-permute-start.26) | collective-permute-done | bytes 393248 | tf_op jit(solution)/shard_map/ppermute | solution.py:41
  152.5 2.1 %shard_map.96.refs_0_ = bf16[1,4,192,2,1024]{4,3,2,1,0:T(2,128)(2,1)} custom-call(s32[1]{0:T(128)} %bitcast.decoder_ref, bf16[192,1024]{1,0:T(8,128)(2,1)S(1)} %copy-done.4, bf16[192,1024]{1,0:T(8,128)(2,1)S(1)} %copy-done.8, bf16[192,1024]{1,0:T(8,128)(2,1)} %collective-permute-done.26.context_ref, ...), custom_call_target="tpu_custom_call", output_to_operand_aliasing={{}: (4, {})} | custom-call | flops 1179648 | bytes 1966080 | tf_op jit(solution)/shard_map/pallas_call | solution.py:236
  154.6 2.0 %collective-permute-done.25.context_ref = bf16[192,512]{1,0:T(8,128)(2,1)S(1)} collective-permute-done((bf16[192,512]{1,0:T(8,128)(2,1)}, bf16[192,512]{1,0:T(8,128)(2,1)S(1)}, u32[]{:S(2)}, u32[]{:S(2)}) %collective-permute-start.25) | collective-permute-done | bytes 196640 | tf_op jit(solution)/shard_map/ppermute | solution.py:41
  157.6 2.2 %collective-permute-done.24.context_ref = bf16[192,512]{1,0:T(8,128)(2,1)} collective-permute-done((bf16[192,512]{1,0:T(8,128)(2,1)}, bf16[192,512]{1,0:T(8,128)(2,1)}, u32[]{:S(2)}, u32[]{:S(2)}) %collective-permute-start.24) | collective-permute-done | bytes 196640 | tf_op jit(solution)/shard_map/ppermute | solution.py:41
  159.8 1.9 %shard_map.98 = bf16[1,4,192,2,1024]{4,3,2,1,0:T(2,128)(2,1)} custom-call(s32[1]{0:T(128)} %bitcast.decoder_ref, bf16[192,512]{1,0:T(8,128)(2,1)S(1)} %copy-done.12, bf16[192,512]{1,0:T(8,128)(2,1)S(1)} %copy-done.16, bf16[192,512]{1,0:T(8,128)(2,1)} %collective-permute-done.24.context_ref, ...), custom_call_target="tpu_custom_call", output_to_operand_aliasing={{}: (4, {})} | custom-call | flops 589824 | bytes 983040 | tf_op jit(solution)/shard_map/pallas_call | solution.py:236
  (88 shorter events, 13.3 us)
Async XLA Ops:
  6.5 73.7 %all-gather.2.cloned.1.call-start = ((), (), s32[]{:S(2)}) async-start(), calls=%async_computation | async-start | bytes 7864320 | tf_op jit(solution)/shard_map/all_gather | solution.py:262
  8.4 15.3 %collective-permute-start.8 = (bf16[128,2048]{1,0:T(8,128)(2,1)S(1)}, bf16[128,2048]{1,0:T(8,128)(2,1)S(1)}, u32[]{:S(2)}, u32[]{:S(2)}) collective-permute-start(bf16[128,2048]{1,0:T(8,128)(2,1)S(1)} %bitcast.7), channel_id=1, source_target_pairs={{0,8},{1,9},{2,10},{3,11},{4,12},{5,13},{6,14},{7,15},{8,0},{9,1},... | collective-permute-start | bytes 1572872 | tf_op jit(solution)/shard_map/ppermute | solution.py:41
  10.8 16.8 %collective-permute-start.6 = (bf16[128,2048]{1,0:T(8,128)(2,1)S(1)}, bf16[128,2048]{1,0:T(8,128)(2,1)S(1)}, u32[]{:S(2)}, u32[]{:S(2)}) collective-permute-start(bf16[128,2048]{1,0:T(8,128)(2,1)S(1)} %bitcast.8), channel_id=1, source_target_pairs={{0,112},{1,113},{2,114},{3,115},{4,116},{5,117},{6,118},{7,119},{8... | collective-permute-start | bytes 1572872 | tf_op jit(solution)/shard_map/ppermute | solution.py:41
  16.7 14.3 %collective-permute-start = (bf16[128,2048]{1,0:T(8,128)(2,1)S(1)}, bf16[128,2048]{1,0:T(8,128)(2,1)S(1)}, u32[]{:S(2)}, u32[]{:S(2)}) collective-permute-start(bf16[128,2048]{1,0:T(8,128)(2,1)S(1)} %bitcast.9), channel_id=1, source_target_pairs={{0,16},{1,17},{2,18},{3,19},{4,20},{5,21},{6,22},{7,23},{8,24},{9,... | collective-permute-start | bytes 1572872 | tf_op jit(solution)/shard_map/ppermute | solution.py:41
  31.0 13.4 %collective-permute-start.2 = (bf16[128,2048]{1,0:T(8,128)(2,1)S(1)}, bf16[128,2048]{1,0:T(8,128)(2,1)S(1)}, u32[]{:S(2)}, u32[]{:S(2)}) collective-permute-start(bf16[128,2048]{1,0:T(8,128)(2,1)S(1)} %collective-permute-done.refs_1_), channel_id=1, source_target_pairs={{0,16},{1,17},{2,18},{3,19},{4,20},{5,21},{6,22},{7,23},{8,24},{9,... | collective-permute-start | bytes 1572872 | tf_op jit(solution)/shard_map/ppermute | solution.py:41
  31.0 13.4 %collective-permute-start.9 = (bf16[128,2048]{1,0:T(8,128)(2,1)S(1)}, bf16[128,2048]{1,0:T(8,128)(2,1)S(1)}, u32[]{:S(2)}, u32[]{:S(2)}) collective-permute-start(bf16[128,2048]{1,0:T(8,128)(2,1)S(1)} %collective-permute-done.6.refs_2_), channel_id=1, source_target_pairs={{0,112},{1,113},{2,114},{3,115},{4,116},{5,117},{6,118},{7,119},{8... | collective-permute-start | bytes 1572872 | tf_op jit(solution)/shard_map/ppermute | solution.py:41
  34.2 16.4 %collective-permute-start.7 = (bf16[128,2048]{1,0:T(8,128)(2,1)S(1)}, bf16[128,2048]{1,0:T(8,128)(2,1)S(1)}, u32[]{:S(2)}, u32[]{:S(2)}) collective-permute-start(bf16[128,2048]{1,0:T(8,128)(2,1)S(1)} %collective-permute-done.6.refs_2_), channel_id=1, source_target_pairs={{0,8},{1,9},{2,10},{3,11},{4,12},{5,13},{6,14},{7,15},{8,0},{9,1},... | collective-permute-start | bytes 1572872 | tf_op jit(solution)/shard_map/ppermute | solution.py:41
  35.4 23.1 %collective-permute-start.1 = (bf16[128,2048]{1,0:T(8,128)(2,1)S(1)}, bf16[128,2048]{1,0:T(8,128)(2,1)S(1)}, u32[]{:S(2)}, u32[]{:S(2)}) collective-permute-start(bf16[128,2048]{1,0:T(8,128)(2,1)S(1)} %collective-permute-done.refs_1_), channel_id=1, source_target_pairs={{0,8},{1,9},{2,10},{3,11},{4,12},{5,13},{6,14},{7,15},{8,0},{9,1},... | collective-permute-start | bytes 1572872 | tf_op jit(solution)/shard_map/ppermute | solution.py:41
  44.4 12.6 %collective-permute-start.3 = (bf16[128,2048]{1,0:T(8,128)(2,1)S(1)}, bf16[128,2048]{1,0:T(8,128)(2,1)S(1)}, u32[]{:S(2)}, u32[]{:S(2)}) collective-permute-start(bf16[128,2048]{1,0:T(8,128)(2,1)S(1)} %collective-permute-done.2.refs_3_), channel_id=1, source_target_pairs={{0,16},{1,17},{2,18},{3,19},{4,20},{5,21},{6,22},{7,23},{8,24},{9,... | collective-permute-start | bytes 1572872 | tf_op jit(solution)/shard_map/ppermute | solution.py:41
  50.6 9.9 %collective-permute-start.10 = (bf16[128,2048]{1,0:T(8,128)(2,1)S(1)}, bf16[128,2048]{1,0:T(8,128)(2,1)S(1)}, u32[]{:S(2)}, u32[]{:S(2)}) collective-permute-start(bf16[128,2048]{1,0:T(8,128)(2,1)S(1)} %collective-permute-done.9.refs_4_), channel_id=1, source_target_pairs={{0,112},{1,113},{2,114},{3,115},{4,116},{5,117},{6,118},{7,119},{8... | collective-permute-start | bytes 1572872 | tf_op jit(solution)/shard_map/ppermute | solution.py:41
  56.9 11.9 %collective-permute-start.4 = (bf16[128,2048]{1,0:T(8,128)(2,1)S(1)}, bf16[128,2048]{1,0:T(8,128)(2,1)}, u32[]{:S(2)}, u32[]{:S(2)}) collective-permute-start(bf16[128,2048]{1,0:T(8,128)(2,1)S(1)} %collective-permute-done.3.refs_0_), channel_id=1, source_target_pairs={{0,16},{1,17},{2,18},{3,19},{4,20},{5,21},{6,22},{7,23},{8,24},{9,... | collective-permute-start | bytes 1572872 | tf_op jit(solution)/shard_map/ppermute | solution.py:41
  60.5 11.1 %collective-permute-start.12 = (bf16[128,2048]{1,0:T(8,128)(2,1)S(1)}, bf16[128,2048]{1,0:T(8,128)(2,1)S(1)}, u32[]{:S(2)}, u32[]{:S(2)}) collective-permute-start(bf16[128,2048]{1,0:T(8,128)(2,1)S(1)} %collective-permute-done.3.refs_0_), channel_id=1, source_target_pairs={{0,8},{1,9},{2,10},{3,11},{4,12},{5,13},{6,14},{7,15},{8,0},{9,1},... | collective-permute-start | bytes 1572872 | tf_op jit(solution)/shard_map/ppermute | solution.py:41
  61.0 11.4 %collective-permute-start.11 = (bf16[128,2048]{1,0:T(8,128)(2,1)S(1)}, bf16[128,2048]{1,0:T(8,128)(2,1)}, u32[]{:S(2)}, u32[]{:S(2)}) collective-permute-start(bf16[128,2048]{1,0:T(8,128)(2,1)S(1)} %collective-permute-done.7.refs_3_), channel_id=1, source_target_pairs={{0,112},{1,113},{2,114},{3,115},{4,116},{5,117},{6,118},{7,119},{8... | collective-permute-start | bytes 1572872 | tf_op jit(solution)/shard_map/ppermute | solution.py:41
  62.4 12.6 %copy-start.24 = (s32[32]{0:T(128)S(1)}, s32[32]{0:T(128)}, u32[]{:S(2)}) copy-start(s32[32]{0:T(128)} %constant.81.clone) | copy-start | bytes 388
  62.5 12.6 %copy-start.25 = (s32[32]{0:T(128)S(1)}, s32[32]{0:T(128)}, u32[]{:S(2)}) copy-start(s32[32]{0:T(128)} %constant.79.clone) | copy-start | bytes 388
  62.5 12.5 %copy-start.26 = (s32[32]{0:T(128)S(1)}, s32[32]{0:T(128)}, u32[]{:S(2)}) copy-start(s32[32]{0:T(128)} %constant.78.clone) | copy-start | bytes 388
  62.5 12.6 %copy-start.23 = (s32[32]{0:T(128)S(1)}, s32[32]{0:T(128)}, u32[]{:S(2)}) copy-start(s32[32]{0:T(128)} %constant.86) | copy-start | bytes 388
  62.5 27.9 %collective-permute-start.16 = (bf16[640,2048]{1,0:T(8,128)(2,1)S(1)}, bf16[640,2048]{1,0:T(8,128)(2,1)}, u32[]{:S(2)}, u32[]{:S(2)}) collective-permute-start(bf16[640,2048]{1,0:T(8,128)(2,1)S(1)} %shard_map.84.refs_3_), channel_id=1, source_target_pairs={{0,4},{1,5},{2,6},{3,7},{4,0},{5,1},{6,2},{7,3},{8,12},{9,13},{10,... | collective-permute-start | bytes 7864328 | tf_op jit(solution)/shard_map/ppermute | solution.py:41
  64.1 16.1 %copy-start.21 = (f32[1,4096]{1,0:T(1,128)S(1)}, f32[1,4096]{1,0:T(1,128)}, u32[]{:S(2)}) copy-start(f32[1,4096]{1,0:T(1,128)} %gain_ref.1) | copy-start | bytes 49156
  64.1 26.2 %collective-permute-start.17 = (bf16[640,2048]{1,0:T(8,128)(2,1)}, bf16[640,2048]{1,0:T(8,128)(2,1)}, u32[]{:S(2)}, u32[]{:S(2)}) collective-permute-start(bf16[640,2048]{1,0:T(8,128)(2,1)} %shard_map.85.refs_5_), channel_id=1, source_target_pairs={{0,4},{1,5},{2,6},{3,7},{4,0},{5,1},{6,2},{7,3},{8,12},{9,13},{10,... | collective-permute-start | bytes 7864328 | tf_op jit(solution)/shard_map/ppermute | solution.py:41
  68.8 18.0 %collective-permute-start.5 = (bf16[128,2048]{1,0:T(8,128)(2,1)S(1)}, bf16[128,2048]{1,0:T(8,128)(2,1)}, u32[]{:S(2)}, u32[]{:S(2)}) collective-permute-start(bf16[128,2048]{1,0:T(8,128)(2,1)S(1)} %collective-permute-done.1.refs_4_), channel_id=1, source_target_pairs={{0,16},{1,17},{2,18},{3,19},{4,20},{5,21},{6,22},{7,23},{8,24},{9,... | collective-permute-start | bytes 1572872 | tf_op jit(solution)/shard_map/ppermute | solution.py:41
  72.4 14.6 %collective-permute-start.14 = (bf16[128,2048]{1,0:T(8,128)(2,1)}, bf16[128,2048]{1,0:T(8,128)(2,1)}, u32[]{:S(2)}, u32[]{:S(2)}) collective-permute-start(bf16[128,2048]{1,0:T(8,128)(2,1)} %collective-permute-done.4.refs_0_), channel_id=1, source_target_pairs={{0,8},{1,9},{2,10},{3,11},{4,12},{5,13},{6,14},{7,15},{8,0},{9,1},... | collective-permute-start | bytes 1572872 | tf_op jit(solution)/shard_map/ppermute | solution.py:41
  74.0 13.0 %collective-permute-start.13 = (bf16[128,2048]{1,0:T(8,128)(2,1)}, bf16[128,2048]{1,0:T(8,128)(2,1)}, u32[]{:S(2)}, u32[]{:S(2)}) collective-permute-start(bf16[128,2048]{1,0:T(8,128)(2,1)} %collective-permute-done.11.refs_1_), channel_id=1, source_target_pairs={{0,112},{1,113},{2,114},{3,115},{4,116},{5,117},{6,118},{7,119},{8... | collective-permute-start | bytes 1572872 | tf_op jit(solution)/shard_map/ppermute | solution.py:41
  86.8 3.5 %collective-permute-start.18 = (bf16[384,2048]{1,0:T(8,128)(2,1)S(1)}, bf16[384,2048]{1,0:T(8,128)(2,1)S(1)}, u32[]{:S(2)}, u32[]{:S(2)}) collective-permute-start(bf16[384,2048]{1,0:T(8,128)(2,1)S(1)} %copy-done.2), channel_id=1, source_target_pairs={{0,4},{1,5},{2,6},{3,7},{4,0},{5,1},{6,2},{7,3},{8,12},{9,13},{10,... | collective-permute-start | bytes 4718600 | tf_op jit(solution)/shard_map/ppermute | solution.py:41
  88.4 4.2 %collective-permute-start.15 = (bf16[384,2048]{1,0:T(8,128)(2,1)S(1)}, bf16[384,2048]{1,0:T(8,128)(2,1)S(1)}, u32[]{:S(2)}, u32[]{:S(2)}) collective-permute-start(bf16[384,2048]{1,0:T(8,128)(2,1)S(1)} %shard_map.83.refs_1_), channel_id=1, source_target_pairs={{0,4},{1,5},{2,6},{3,7},{4,0},{5,1},{6,2},{7,3},{8,12},{9,13},{10,... | collective-permute-start | bytes 4718600 | tf_op jit(solution)/shard_map/ppermute | solution.py:41
  101.9 21.1 %copy-start.5 = (bf16[192,1024]{1,0:T(8,128)(2,1)}, bf16[192,1024]{1,0:T(8,128)(2,1)S(1)}, u32[]{:S(2)}) copy-start(bf16[192,1024]{1,0:T(8,128)(2,1)S(1)} %get-tuple-element.35.k_ref.front_ref) | copy-start | bytes 1179652
  101.9 28.9 %copy-start.3 = (bf16[192,1024]{1,0:T(8,128)(2,1)}, bf16[192,1024]{1,0:T(8,128)(2,1)S(1)}, u32[]{:S(2)}) copy-start(bf16[192,1024]{1,0:T(8,128)(2,1)S(1)} %get-tuple-element.34.k_ref.front_ref) | copy-start | bytes 1179652
  101.9 36.5 %copy-start.13 = (bf16[192,512]{1,0:T(8,128)(2,1)}, bf16[192,512]{1,0:T(8,128)(2,1)S(1)}, u32[]{:S(2)}) copy-start(bf16[192,512]{1,0:T(8,128)(2,1)S(1)} %get-tuple-element.33.k_ref.front_ref) | copy-start | bytes 589828
  101.9 40.7 %copy-start.11 = (bf16[192,512]{1,0:T(8,128)(2,1)}, bf16[192,512]{1,0:T(8,128)(2,1)S(1)}, u32[]{:S(2)}) copy-start(bf16[192,512]{1,0:T(8,128)(2,1)S(1)} %get-tuple-element.31.k_ref.front_ref) | copy-start | bytes 589828
  101.9 17.2 %collective-permute-start.23 = (bf16[192,1024]{1,0:T(8,128)(2,1)S(1)}, bf16[192,1024]{1,0:T(8,128)(2,1)S(1)}, u32[]{:S(2)}, u32[]{:S(2)}) collective-permute-start(bf16[192,1024]{1,0:T(8,128)(2,1)S(1)} %get-tuple-element.36.k_ref.front_ref), channel_id=1, source_target_pairs={{128,0},{129,1},{130,2},{131,3},{132,4},{133,5},{134,6},{135,7},{1... | collective-permute-start | bytes 1179656 | tf_op jit(solution)/shard_map/ppermute | solution.py:41
  104.5 18.4 %collective-permute-start.22 = (bf16[192,1024]{1,0:T(8,128)(2,1)S(1)}, bf16[192,1024]{1,0:T(8,128)(2,1)S(1)}, u32[]{:S(2)}, u32[]{:S(2)}) collective-permute-start(bf16[192,1024]{1,0:T(8,128)(2,1)S(1)} %get-tuple-element.35.k_ref.front_ref), channel_id=1, source_target_pairs={{128,0},{129,1},{130,2},{131,3},{132,4},{133,5},{134,6},{135,7},{1... | collective-permute-start | bytes 1179656 | tf_op jit(solution)/shard_map/ppermute | solution.py:41
  105.8 25.0 %collective-permute-start.21 = (bf16[192,1024]{1,0:T(8,128)(2,1)S(1)}, bf16[192,1024]{1,0:T(8,128)(2,1)S(1)}, u32[]{:S(2)}, u32[]{:S(2)}) collective-permute-start(bf16[192,1024]{1,0:T(8,128)(2,1)S(1)} %get-tuple-element.34.k_ref.front_ref), channel_id=1, source_target_pairs={{128,0},{129,1},{130,2},{131,3},{132,4},{133,5},{134,6},{135,7},{1... | collective-permute-start | bytes 1179656 | tf_op jit(solution)/shard_map/ppermute | solution.py:41
  107.1 35.5 %collective-permute-start.19 = (bf16[192,512]{1,0:T(8,128)(2,1)S(1)}, bf16[192,512]{1,0:T(8,128)(2,1)S(1)}, u32[]{:S(2)}, u32[]{:S(2)}) collective-permute-start(bf16[192,512]{1,0:T(8,128)(2,1)S(1)} %get-tuple-element.31.k_ref.front_ref), channel_id=1, source_target_pairs={{128,0},{129,1},{130,2},{131,3},{132,4},{133,5},{134,6},{135,7},{1... | collective-permute-start | bytes 589832 | tf_op jit(solution)/shard_map/ppermute | solution.py:41
  108.5 10.7 %copy-start.22 = (s32[4,1]{0,1:T(1,128)S(1)}, s32[4,1]{0,1:T(1,128)}, u32[]{:S(2)}) copy-start(s32[4,1]{0,1:T(1,128)} %param.11) | copy-start | bytes 52
  108.5 29.9 %collective-permute-start.20 = (bf16[192,512]{1,0:T(8,128)(2,1)S(1)}, bf16[192,512]{1,0:T(8,128)(2,1)S(1)}, u32[]{:S(2)}, u32[]{:S(2)}) collective-permute-start(bf16[192,512]{1,0:T(8,128)(2,1)S(1)} %get-tuple-element.33.k_ref.front_ref), channel_id=1, source_target_pairs={{128,0},{129,1},{130,2},{131,3},{132,4},{133,5},{134,6},{135,7},{1... | collective-permute-start | bytes 589832 | tf_op jit(solution)/shard_map/ppermute | solution.py:41
  119.1 21.8 %copy-start.7 = (bf16[192,1024]{1,0:T(8,128)(2,1)}, bf16[192,1024]{1,0:T(8,128)(2,1)S(1)}, u32[]{:S(2)}) copy-start(bf16[192,1024]{1,0:T(8,128)(2,1)S(1)} %get-tuple-element.41.v_ref.back_ref) | copy-start | bytes 1179652
  119.1 21.8 %copy-start.9 = (bf16[192,1024]{1,0:T(8,128)(2,1)}, bf16[192,1024]{1,0:T(8,128)(2,1)S(1)}, u32[]{:S(2)}) copy-start(bf16[192,1024]{1,0:T(8,128)(2,1)S(1)} %get-tuple-element.39.v_ref.back_ref) | copy-start | bytes 1179652
  119.1 21.8 %copy-start.17 = (bf16[192,512]{1,0:T(8,128)(2,1)}, bf16[192,512]{1,0:T(8,128)(2,1)S(1)}, u32[]{:S(2)}) copy-start(bf16[192,512]{1,0:T(8,128)(2,1)S(1)} %get-tuple-element.43.v_ref.back_ref) | copy-start | bytes 589828
  119.1 23.5 %copy-start.15 = (bf16[192,512]{1,0:T(8,128)(2,1)}, bf16[192,512]{1,0:T(8,128)(2,1)S(1)}, u32[]{:S(2)}) copy-start(bf16[192,512]{1,0:T(8,128)(2,1)S(1)} %get-tuple-element.32.v_ref.back_ref) | copy-start | bytes 589828
  121.6 24.8 %collective-permute-start.28 = (bf16[192,1024]{1,0:T(8,128)(2,1)S(1)}, bf16[192,1024]{1,0:T(8,128)(2,1)S(1)}, u32[]{:S(2)}, u32[]{:S(2)}) collective-permute-start(bf16[192,1024]{1,0:T(8,128)(2,1)S(1)} %shard_map.89), channel_id=1, source_target_pairs={{0,128},{1,129},{2,130},{3,131},{4,132},{5,133},{6,134},{7,135},{8... | collective-permute-start | bytes 1179656 | tf_op jit(solution)/shard_map/ppermute | solution.py:41
  125.4 22.3 %collective-permute-start.27 = (bf16[192,1024]{1,0:T(8,128)(2,1)S(1)}, bf16[192,1024]{1,0:T(8,128)(2,1)}, u32[]{:S(2)}, u32[]{:S(2)}) collective-permute-start(bf16[192,1024]{1,0:T(8,128)(2,1)S(1)} %shard_map.90), channel_id=1, source_target_pairs={{0,128},{1,129},{2,130},{3,131},{4,132},{5,133},{6,134},{7,135},{8... | collective-permute-start | bytes 1179656 | tf_op jit(solution)/shard_map/ppermute | solution.py:41
  133.2 19.2 %collective-permute-start.26 = (bf16[192,1024]{1,0:T(8,128)(2,1)S(1)}, bf16[192,1024]{1,0:T(8,128)(2,1)}, u32[]{:S(2)}, u32[]{:S(2)}) collective-permute-start(bf16[192,1024]{1,0:T(8,128)(2,1)S(1)} %shard_map.91), channel_id=1, source_target_pairs={{0,128},{1,129},{2,130},{3,131},{4,132},{5,133},{6,134},{7,135},{8... | collective-permute-start | bytes 1179656 | tf_op jit(solution)/shard_map/ppermute | solution.py:41
  140.9 6.7 %copy-start.6 = (bf16[192,1024]{1,0:T(8,128)(2,1)S(1)}, bf16[192,1024]{1,0:T(8,128)(2,1)}, u32[]{:S(2)}) copy-start(bf16[192,1024]{1,0:T(8,128)(2,1)} %copy-done.5) | copy-start | bytes 1179652
  140.9 15.6 %collective-permute-start.25 = (bf16[192,512]{1,0:T(8,128)(2,1)}, bf16[192,512]{1,0:T(8,128)(2,1)S(1)}, u32[]{:S(2)}, u32[]{:S(2)}) collective-permute-start(bf16[192,512]{1,0:T(8,128)(2,1)} %shard_map.92), channel_id=1, source_target_pairs={{0,128},{1,129},{2,130},{3,131},{4,132},{5,133},{6,134},{7,135},{8... | collective-permute-start | bytes 589832 | tf_op jit(solution)/shard_map/ppermute | solution.py:41
  145.2 14.6 %collective-permute-start.24 = (bf16[192,512]{1,0:T(8,128)(2,1)}, bf16[192,512]{1,0:T(8,128)(2,1)}, u32[]{:S(2)}, u32[]{:S(2)}) collective-permute-start(bf16[192,512]{1,0:T(8,128)(2,1)} %shard_map.93), channel_id=1, source_target_pairs={{0,128},{1,129},{2,130},{3,131},{4,132},{5,133},{6,134},{7,135},{8... | collective-permute-start | bytes 589832 | tf_op jit(solution)/shard_map/ppermute | solution.py:41
  149.9 6.7 %copy-start.14 = (bf16[192,512]{1,0:T(8,128)(2,1)S(1)}, bf16[192,512]{1,0:T(8,128)(2,1)}, u32[]{:S(2)}) copy-start(bf16[192,512]{1,0:T(8,128)(2,1)} %copy-done.13) | copy-start | bytes 589828
  149.9 6.7 %copy-start.18 = (bf16[192,512]{1,0:T(8,128)(2,1)S(1)}, bf16[192,512]{1,0:T(8,128)(2,1)}, u32[]{:S(2)}) copy-start(bf16[192,512]{1,0:T(8,128)(2,1)} %copy-done.17) | copy-start | bytes 589828
  154.6 5.2 %copy-start.16 = (bf16[192,512]{1,0:T(8,128)(2,1)S(1)}, bf16[192,512]{1,0:T(8,128)(2,1)}, u32[]{:S(2)}) copy-start(bf16[192,512]{1,0:T(8,128)(2,1)} %copy-done.15) | copy-start | bytes 589828
  (9 other events, 29.6 us)
Sparse Core Ops, SparseCore 0:
  9.2 71.0 all-gather.1

commit v3 on v2

--- a/solution.py
+++ b/solution.py
@@ -143,11 +143,14 @@
         row += count
 
 
-def matmul(xs, x_block, start, parts, base, dtype, width, column, tile, pieces, mib, weight=1):
-    tokens = sum(x.shape[0] for x in xs)
+def matmul(xs, x_block, start, parts, base, dtype, width, column, tile, pieces, mib, weight=1, part=(0, 1)):
+    chosen, count = part
+    tokens = sum(x.shape[0] for x in xs) // count
     depths = [p.shape[0] for p in parts]
     first = column // tile
-    in_specs = [pl.BlockSpec((x.shape[0], x_block), lambda j: (0, 0), pipeline_mode=pl.Buffered(1)) for x in xs]
+    in_specs = [
+        pl.BlockSpec((x.shape[0] // count, x_block), lambda j: (chosen, 0), pipeline_mode=pl.Buffered(1)) for x in xs
+    ]
     in_specs += [pl.BlockSpec((d, tile), lambda j: (0, first + j)) for d in depths]
     args = [*xs, *parts]
     if base is not None:
@@ -294,16 +297,25 @@
     pieces += [(tokens - tok, tokens, 0, wide // 2), (tokens - tok, tokens, wide // 2, wide)]
     front = matmul(normed, 4096, 0, bundles, None, jnp.bfloat16, wide, 0, 256, pieces, 20)
     queries = [sent(piece, TO_ENC) for piece in front]
-    back = matmul(normed, 4096, 0, bundles, None, jnp.bfloat16, wide, wide, 256, pieces, 20, 0)
+    def back_of(x, part, pieces):
+        return matmul((x,), 4096, 0, bundles, None, jnp.bfloat16, wide, wide, 256, pieces, 20, 0, (part, 2))
+
+    front, half = list(front), tokens // 2
+    back = back_of(normed[0], 0, [p for p in pieces if p[1] <= half])
 
     limit = lengths.reshape(batch)
     shape = (1, batch, tok, 2, wide)
     out, context = None, None
-    for (low, _, column, _), query, f, b in zip(pieces, queries, front, back):
+    for k, (low, _, column, _) in enumerate(pieces):
+        query = queries[k]
         if context is not None:
             query = after(query, context)
-        context = attend(low // tok, limit, query, f, b)
-        out = finish(low // tok, column, shape, decoder, f, b, sent(context, TO_DEC), out)
+        if k == 1:
+            rest = [(p[0] - half, p[1] - half, *p[2:]) for p in pieces if p[0] >= half]
+            back = [*back, *back_of(after(normed[0], context), 1, rest)]
+            front[1] = after(front[1], *back)
+        context = attend(low // tok, limit, query, front[k], back[k])
+        out = finish(low // tok, column, shape, decoder, front[k], back[k], sent(context, TO_DEC), out)
     return out
 
 

time: 169 us -> 169 us (level)
  waiting for transfers between devices: 64 us -> 54.8 us
  starting transfers between devices: 35.3 us -> 41.7 us
  Pallas kernels: 47.4 us -> 49.7 us
    ppermute x29, waiting for transfers between devices: 62.3 us -> 53 us  [sent(): return lax.ppermute(x, AXES, pairs)]
    ppermute x29, starting transfers between devices: 35.3 us -> 41.7 us  [sent(): return lax.ppermute(x, AXES, pairs)]
    pallas_call x2 -> x3, Pallas kernels: 18.6 us -> 21.1 us  [matmul(): pl.pallas_call(functools.partial(matmul_kernel, start, len(xs), len(parts...]
  transfers between devices with their start and end apart: 30 -> 30, of which waited for: 18 -> 17; matrix products, arithmetic and copies ran while one was open for 1% -> 1% of each run, Pallas kernels for 22% -> 23%
where the time goes in v3:
time: 169 us; the launch traced here: 168 us
  waiting for transfers between devices  54.8 us (32%)
  Pallas kernels  49.7 us (29%)
  starting transfers between devices  41.7 us (25%)
  between operations  13.9 us (8%)
  local copies, waits for them, and re-layouts  7.82 us (5%)
    ppermute x29, waiting for transfers between devices, sent(): return lax.ppermute(x, AXES, pairs)  53 us
    ppermute x29, starting transfers between devices, sent(): return lax.ppermute(x, AXES, pairs)  41.7 us
    pallas_call x3, Pallas kernels, matmul(): pl.pallas_call(functools.partial(matmul_kernel, start, len(xs), len(parts...  21.1 us
    pallas_call x5, Pallas kernels, attend(): pl.pallas_call(functools.partial(attend_kernel, index), grid_spec=pltpu.P...  13.1 us
    pallas_call x5, Pallas kernels, finish(): pl.pallas_call(finish_kernel, grid_spec=pltpu.PrefetchScalarGridSpec(num_...  7.34 us
    unnamed x55, local copies, waits for them, and re-layouts  7.12 us
    pallas_call x4, Pallas kernels, stacked(): pl.pallas_call(stack_kernel, in_specs=[pl.BlockSpec(memory_space=pl.ANY)]...  4.37 us
    pallas_call x1, Pallas kernels, norm(): pl.pallas_call(functools.partial(norm_kernel, 32), grid_spec=pltpu.Prefet...  3.76 us
  transfers between devices with their start and end apart: 30, of which 17 were waited for; matrix products, arithmetic and copies ran while one was open for 1% of the time, Pallas kernels for 23%

profile of v3, /device:TPU:8, one launch (start us, length us, event | category | flops | bytes accessed | tf_op | source)
XLA Modules:
  0.0 167.9 jit_solution(8398669182094693956)
XLA Ops:
  8.4 5.9 %collective-permute-start.6 = (bf16[128,2048]{1,0:T(8,128)(2,1)S(1)}, bf16[128,2048]{1,0:T(8,128)(2,1)S(1)}, u32[]{:S(2)}, u32[]{:S(2)}) collective-permute-start(bf16[128,2048]{1,0:T(8,128)(2,1)S(1)} %bitcast.7), channel_id=1, source_target_pairs={{0,112},{1,113},{2,114},{3,115},{4,116},{5,117},{6,118},{7,119},{8... | collective-permute-start | bytes 1572872 | tf_op jit(solution)/shard_map/ppermute | solution.py:41
  14.3 2.3 %collective-permute-start.8 = (bf16[128,2048]{1,0:T(8,128)(2,1)S(1)}, bf16[128,2048]{1,0:T(8,128)(2,1)S(1)}, u32[]{:S(2)}, u32[]{:S(2)}) collective-permute-start(bf16[128,2048]{1,0:T(8,128)(2,1)S(1)} %bitcast.8), channel_id=1, source_target_pairs={{0,8},{1,9},{2,10},{3,11},{4,12},{5,13},{6,14},{7,15},{8,0},{9,1},... | collective-permute-start | bytes 1572872 | tf_op jit(solution)/shard_map/ppermute | solution.py:41
  16.6 8.9 %collective-permute-done.6.refs_2_ = bf16[128,2048]{1,0:T(8,128)(2,1)S(1)} collective-permute-done((bf16[128,2048]{1,0:T(8,128)(2,1)S(1)}, bf16[128,2048]{1,0:T(8,128)(2,1)S(1)}, u32[]{:S(2)}, u32[]{:S(2)}) %collective-permute-start.6) | collective-permute-done | bytes 524320 | tf_op jit(solution)/shard_map/ppermute | solution.py:41
  25.5 3.7 %collective-permute-done.8.refs_2_ = bf16[128,2048]{1,0:T(8,128)(2,1)S(1)} collective-permute-done((bf16[128,2048]{1,0:T(8,128)(2,1)S(1)}, bf16[128,2048]{1,0:T(8,128)(2,1)S(1)}, u32[]{:S(2)}, u32[]{:S(2)}) %collective-permute-start.8) | collective-permute-done | bytes 524320 | tf_op jit(solution)/shard_map/ppermute | solution.py:41
  29.2 1.7 %collective-permute-done.refs_1_ = bf16[128,2048]{1,0:T(8,128)(2,1)S(1)} collective-permute-done((bf16[128,2048]{1,0:T(8,128)(2,1)S(1)}, bf16[128,2048]{1,0:T(8,128)(2,1)S(1)}, u32[]{:S(2)}, u32[]{:S(2)}) %collective-permute-start) | collective-permute-done | bytes 524320 | tf_op jit(solution)/shard_map/ppermute | solution.py:41
  31.0 1.2 collective-permute-start.7
  32.2 3.2 %collective-permute-start.9 = (bf16[128,2048]{1,0:T(8,128)(2,1)S(1)}, bf16[128,2048]{1,0:T(8,128)(2,1)S(1)}, u32[]{:S(2)}, u32[]{:S(2)}) collective-permute-start(bf16[128,2048]{1,0:T(8,128)(2,1)S(1)} %collective-permute-done.6.refs_2_), channel_id=1, source_target_pairs={{0,112},{1,113},{2,114},{3,115},{4,116},{5,117},{6,118},{7,119},{8... | collective-permute-start | bytes 1572872 | tf_op jit(solution)/shard_map/ppermute | solution.py:41
  35.4 2.3 %collective-permute-start.1 = (bf16[128,2048]{1,0:T(8,128)(2,1)S(1)}, bf16[128,2048]{1,0:T(8,128)(2,1)S(1)}, u32[]{:S(2)}, u32[]{:S(2)}) collective-permute-start(bf16[128,2048]{1,0:T(8,128)(2,1)S(1)} %collective-permute-done.refs_1_), channel_id=1, source_target_pairs={{0,8},{1,9},{2,10},{3,11},{4,12},{5,13},{6,14},{7,15},{8,0},{9,1},... | collective-permute-start | bytes 1572872 | tf_op jit(solution)/shard_map/ppermute | solution.py:41
  37.7 6.6 %collective-permute-done.2.refs_3_ = bf16[128,2048]{1,0:T(8,128)(2,1)S(1)} collective-permute-done((bf16[128,2048]{1,0:T(8,128)(2,1)S(1)}, bf16[128,2048]{1,0:T(8,128)(2,1)S(1)}, u32[]{:S(2)}, u32[]{:S(2)}) %collective-permute-start.2) | collective-permute-done | bytes 524320 | tf_op jit(solution)/shard_map/ppermute | solution.py:41
  44.4 3.0 %collective-permute-done.7.refs_3_ = bf16[128,2048]{1,0:T(8,128)(2,1)S(1)} collective-permute-done((bf16[128,2048]{1,0:T(8,128)(2,1)S(1)}, bf16[128,2048]{1,0:T(8,128)(2,1)S(1)}, u32[]{:S(2)}, u32[]{:S(2)}) %collective-permute-start.7) | collective-permute-done | bytes 524320 | tf_op jit(solution)/shard_map/ppermute | solution.py:41
  47.3 3.2 %collective-permute-start.10 = (bf16[128,2048]{1,0:T(8,128)(2,1)S(1)}, bf16[128,2048]{1,0:T(8,128)(2,1)S(1)}, u32[]{:S(2)}, u32[]{:S(2)}) collective-permute-start(bf16[128,2048]{1,0:T(8,128)(2,1)S(1)} %collective-permute-done.9.refs_4_), channel_id=1, source_target_pairs={{0,112},{1,113},{2,114},{3,115},{4,116},{5,117},{6,118},{7,119},{8... | collective-permute-start | bytes 1572872 | tf_op jit(solution)/shard_map/ppermute | solution.py:41
  50.6 6.4 %collective-permute-done.3.refs_0_ = bf16[128,2048]{1,0:T(8,128)(2,1)S(1)} collective-permute-done((bf16[128,2048]{1,0:T(8,128)(2,1)S(1)}, bf16[128,2048]{1,0:T(8,128)(2,1)S(1)}, u32[]{:S(2)}, u32[]{:S(2)}) %collective-permute-start.3) | collective-permute-done | bytes 524320 | tf_op jit(solution)/shard_map/ppermute | solution.py:41
  57.7 3.7 %collective-permute-start.11 = (bf16[128,2048]{1,0:T(8,128)(2,1)S(1)}, bf16[128,2048]{1,0:T(8,128)(2,1)}, u32[]{:S(2)}, u32[]{:S(2)}) collective-permute-start(bf16[128,2048]{1,0:T(8,128)(2,1)S(1)} %collective-permute-done.7.refs_3_), channel_id=1, source_target_pairs={{0,112},{1,113},{2,114},{3,115},{4,116},{5,117},{6,118},{7,119},{8... | collective-permute-start | bytes 1572872 | tf_op jit(solution)/shard_map/ppermute | solution.py:41
  61.4 2.0 %collective-permute-start.12 = (bf16[128,2048]{1,0:T(8,128)(2,1)S(1)}, bf16[128,2048]{1,0:T(8,128)(2,1)S(1)}, u32[]{:S(2)}, u32[]{:S(2)}) collective-permute-start(bf16[128,2048]{1,0:T(8,128)(2,1)S(1)} %collective-permute-done.3.refs_0_), channel_id=1, source_target_pairs={{0,8},{1,9},{2,10},{3,11},{4,12},{5,13},{6,14},{7,15},{8,0},{9,1},... | collective-permute-start | bytes 1572872 | tf_op jit(solution)/shard_map/ppermute | solution.py:41
  63.8 1.5 shard_map.85.refs_5_
  65.9 2.8 %collective-permute-done.4.refs_0_ = bf16[128,2048]{1,0:T(8,128)(2,1)} collective-permute-done((bf16[128,2048]{1,0:T(8,128)(2,1)S(1)}, bf16[128,2048]{1,0:T(8,128)(2,1)}, u32[]{:S(2)}, u32[]{:S(2)}) %collective-permute-start.4) | collective-permute-done | bytes 524320 | tf_op jit(solution)/shard_map/ppermute | solution.py:41
  68.8 3.3 %collective-permute-done.12.refs_2_ = bf16[128,2048]{1,0:T(8,128)(2,1)S(1)} collective-permute-done((bf16[128,2048]{1,0:T(8,128)(2,1)S(1)}, bf16[128,2048]{1,0:T(8,128)(2,1)S(1)}, u32[]{:S(2)}, u32[]{:S(2)}) %collective-permute-start.12) | collective-permute-done | bytes 524320 | tf_op jit(solution)/shard_map/ppermute | solution.py:41
  73.1 1.8 %collective-permute-start.14 = (bf16[128,2048]{1,0:T(8,128)(2,1)}, bf16[128,2048]{1,0:T(8,128)(2,1)}, u32[]{:S(2)}, u32[]{:S(2)}) collective-permute-start(bf16[128,2048]{1,0:T(8,128)(2,1)} %collective-permute-done.4.refs_0_), channel_id=1, source_target_pairs={{0,8},{1,9},{2,10},{3,11},{4,12},{5,13},{6,14},{7,15},{8,0},{9,1},... | collective-permute-start | bytes 1572872 | tf_op jit(solution)/shard_map/ppermute | solution.py:41
  76.7 1.2 shard_map.86.refs_7_
  80.3 2.8 %copy-done.2 = bf16[1,4,192,4096]{3,2,1,0:T(8,128)(2,1)S(1)} copy-done((bf16[1,4,192,4096]{3,2,1,0:T(8,128)(2,1)S(1)}, bf16[1,4,192,4096]{3,2,1,0:T(8,128)(2,1)}, u32[]{:S(2)}) %copy-start.2) | copy-done | bytes 6291480
  83.1 3.8 %shard_map.82.refs_0_ = bf16[768,4096]{1,0:T(8,128)(2,1)S(1)} custom-call(s32[32]{0:T(128)S(1)} %gather_fusion, f32[1,4096]{1,0:T(1,128)S(1)} %copy-done.21, bf16[768,4096]{1,0:T(8,128)(2,1)S(1)} %bitcast.6), custom_call_target="tpu_custom_call" | custom-call | flops 18874368 | bytes 12582912 | tf_op jit(solution)/shard_map/pallas_call | solution.py:103
  87.0 1.4 shard_map.83.refs_1_
  88.9 1.4 collective-permute-done.18.refs_8_
  90.3 2.2 %collective-permute-done.15.refs_2_ = bf16[384,2048]{1,0:T(8,128)(2,1)S(1)} collective-permute-done((bf16[384,2048]{1,0:T(8,128)(2,1)S(1)}, bf16[384,2048]{1,0:T(8,128)(2,1)S(1)}, u32[]{:S(2)}, u32[]{:S(2)}) %collective-permute-start.15) | collective-permute-done | bytes 1572896 | tf_op jit(solution)/shard_map/ppermute | solution.py:41
  92.6 9.3 %shard_map.87 = (bf16[192,1024]{1,0:T(8,128)(2,1)S(1)}, bf16[192,1024]{1,0:T(8,128)(2,1)S(1)}, bf16[192,1024]{1,0:T(8,128)(2,1)S(1)}, bf16[192,512]{1,0:T(8,128)(2,1)S(1)}, bf16[192,512]{1,0:T(8,128)(2,1)S(1)}) custom-call(bf16[768,4096]{1,0:T(8,128)(2,1)S(1)} %shard_map.82.refs_0_, bf16[384,2048]{1,0:T(8,128)(2,1)S(1)} %shard_map.83.refs_1_, ...), custom_call_target="tpu_custom_call" | custom-call | flops 6442450944 | bytes 19398656 | tf_op jit(solution)/shard_map/pallas_call | solution.py:163
  101.9 2.5 %collective-permute-start.19 = (bf16[192,1024]{1,0:T(8,128)(2,1)S(1)}, bf16[192,1024]{1,0:T(8,128)(2,1)S(1)}, u32[]{:S(2)}, u32[]{:S(2)}) collective-permute-start(bf16[192,1024]{1,0:T(8,128)(2,1)S(1)} %get-tuple-element.34.k_ref.front_ref), channel_id=1, source_target_pairs={{128,0},{129,1},{130,2},{131,3},{132,4},{133,5},{134,6},{135,7},{1... | collective-permute-start | bytes 1179656 | tf_op jit(solution)/shard_map/ppermute | solution.py:41
  104.4 1.3 collective-permute-start.23
  105.7 1.3 collective-permute-start.22
  107.0 1.3 collective-permute-start.20
  108.4 1.3 collective-permute-start.21
  109.7 5.9 %shard_map.88 = (bf16[192,1024]{1,0:T(8,128)(2,1)S(1)}, bf16[192,1024]{1,0:T(8,128)(2,1)S(1)}) custom-call(bf16[768,4096]{1,0:T(8,128)(2,1)S(1)} %shard_map.82.refs_0_, bf16[384,2048]{1,0:T(8,128)(2,1)S(1)} %shard_map.83.refs_1_, bf16[384,2048]{1,0:T(8,128)(2,1)S(1)} %collective-permute-done.15.refs_2_, bf16[640,2048]{1,0:T(8,128)(2,1)S(1)} %shard_map.84.refs_3_, ...), custom_call_target="tpu_custom_call" | custom-call | tf_op jit(solution)/shard_map/pallas_call | solution.py:163
  115.6 3.2 %shard_map.89 = bf16[192,1024]{1,0:T(8,128)(2,1)} custom-call(s32[4]{0:T(128)S(1)} %bitcast.11, bf16[192,1024]{1,0:T(8,128)(2,1)S(1)} %collective-permute-done.19.q_ref, bf16[192,1024]{1,0:T(8,128)(2,1)S(1)} %get-tuple-element.34.k_ref.front_ref, bf16[192,1024]{1,0:T(8,128)(2,1)S(1)} %get-tuple-element.35.v_ref.back_ref), custom_call_target="tpu_custom_call" | custom-call | flops 301989888 | bytes 1572864 | tf_op jit(solution)/shard_map/pallas_call | solution.py:202
  118.8 1.3 collective-permute-start.28
  120.1 2.2 %collective-permute-done.23.q_ref = bf16[192,1024]{1,0:T(8,128)(2,1)S(1)} collective-permute-done((bf16[192,1024]{1,0:T(8,128)(2,1)S(1)}, bf16[192,1024]{1,0:T(8,128)(2,1)S(1)}, u32[]{:S(2)}, u32[]{:S(2)}) %collective-permute-start.23) | collective-permute-done | bytes 393248 | tf_op jit(solution)/shard_map/ppermute | solution.py:41
  122.3 5.9 %shard_map.90 = (bf16[192,1024]{1,0:T(8,128)(2,1)S(1)}, bf16[192,512]{1,0:T(8,128)(2,1)S(1)}, bf16[192,512]{1,0:T(8,128)(2,1)S(1)}) custom-call(bf16[768,4096]{1,0:T(8,128)(2,1)S(1)} %shard_map.82.refs_0_, bf16[384,2048]{1,0:T(8,128)(2,1)S(1)} %shard_map.83.refs_1_, bf16[384,2048]{1,0:T(8,128)(2,1)S(1)} %collective-permute-done.15.refs_2_, ...), custom_call_target="tpu_custom_call" | custom-call | tf_op jit(solution)/shard_map/pallas_call | solution.py:163
  128.2 2.4 %shard_map.91 = bf16[192,1024]{1,0:T(8,128)(2,1)S(1)} custom-call(s32[4]{0:T(128)S(1)} %bitcast.12, bf16[192,1024]{1,0:T(8,128)(2,1)S(1)} %collective-permute-done.23.q_ref, bf16[192,1024]{1,0:T(8,128)(2,1)S(1)} %get-tuple-element.45.k_ref.front_ref, bf16[192,1024]{1,0:T(8,128)(2,1)S(1)} %get-tuple-element.42.v_ref.back_ref), custom_call_target="tpu_custom_call" | custom-call | flops 301989888 | bytes 1572864 | tf_op jit(solution)/shard_map/pallas_call | solution.py:202
  130.7 1.3 collective-permute-start.27
  132.0 2.4 %shard_map.92 = bf16[192,1024]{1,0:T(8,128)(2,1)S(1)} custom-call(s32[4]{0:T(128)S(1)} %bitcast.13, bf16[192,1024]{1,0:T(8,128)(2,1)S(1)} %collective-permute-done.22.q_ref, bf16[192,1024]{1,0:T(8,128)(2,1)S(1)} %get-tuple-element.39.k_ref.front_ref, bf16[192,1024]{1,0:T(8,128)(2,1)S(1)} %get-tuple-element.43.v_ref.back_ref), custom_call_target="tpu_custom_call" | custom-call | flops 301989888 | bytes 1572864 | tf_op jit(solution)/shard_map/pallas_call | solution.py:202
  134.5 1.5 collective-permute-start.26
  136.0 2.3 %collective-permute-done.21.q_ref = bf16[192,512]{1,0:T(8,128)(2,1)S(1)} collective-permute-done((bf16[192,512]{1,0:T(8,128)(2,1)S(1)}, bf16[192,512]{1,0:T(8,128)(2,1)S(1)}, u32[]{:S(2)}, u32[]{:S(2)}) %collective-permute-start.21) | collective-permute-done | bytes 196640 | tf_op jit(solution)/shard_map/ppermute | solution.py:41
  138.3 2.5 %shard_map.93 = bf16[192,512]{1,0:T(8,128)(2,1)} custom-call(s32[4]{0:T(128)S(1)} %bitcast.14, bf16[192,512]{1,0:T(8,128)(2,1)S(1)} %collective-permute-done.21.q_ref, bf16[192,512]{1,0:T(8,128)(2,1)S(1)} %get-tuple-element.38.k_ref.front_ref, bf16[192,512]{1,0:T(8,128)(2,1)S(1)} %get-tuple-element.44.v_ref.back_ref), custom_call_target="tpu_custom_call" | custom-call | flops 150994944 | bytes 786432 | tf_op jit(solution)/shard_map/pallas_call | solution.py:202
  140.8 1.4 collective-permute-start.25
  142.3 2.5 %shard_map.94 = bf16[192,512]{1,0:T(8,128)(2,1)} custom-call(s32[4]{0:T(128)S(1)} %bitcast.15, bf16[192,512]{1,0:T(8,128)(2,1)S(1)} %collective-permute-done.20.q_ref, bf16[192,512]{1,0:T(8,128)(2,1)S(1)} %get-tuple-element.33.k_ref.front_ref, bf16[192,512]{1,0:T(8,128)(2,1)S(1)} %get-tuple-element.37.v_ref.back_ref), custom_call_target="tpu_custom_call" | custom-call | flops 150994944 | bytes 786432 | tf_op jit(solution)/shard_map/pallas_call | solution.py:202
  144.8 1.3 collective-permute-start.24
  146.1 2.1 %shard_map.95.refs_0_ = bf16[1,4,192,2,1024]{4,3,2,1,0:T(2,128)(2,1)} custom-call(s32[1]{0:T(128)} %bitcast.decoder_ref, bf16[192,1024]{1,0:T(8,128)(2,1)S(1)} %get-tuple-element.34.k_ref.front_ref, bf16[192,1024]{1,0:T(8,128)(2,1)S(1)} %get-tuple-element.35.v_ref.back_ref, bf16[192,1024]{1,0:T(8,128)(2,1)} %collective-permute-done.28.context_ref), custom_call_target="tpu_custom_call" | custom-call | flops 1179648 | bytes 1966080 | tf_op jit(solution)/shard_map/pallas_call | solution.py:239
  149.5 3.6 %collective-permute-done.26.context_ref = bf16[192,1024]{1,0:T(8,128)(2,1)S(1)} collective-permute-done((bf16[192,1024]{1,0:T(8,128)(2,1)S(1)}, bf16[192,1024]{1,0:T(8,128)(2,1)S(1)}, u32[]{:S(2)}, u32[]{:S(2)}) %collective-permute-start.26) | collective-permute-done | bytes 393248 | tf_op jit(solution)/shard_map/ppermute | solution.py:41
  154.2 2.7 %collective-permute-done.25.context_ref = bf16[192,512]{1,0:T(8,128)(2,1)S(1)} collective-permute-done((bf16[192,512]{1,0:T(8,128)(2,1)}, bf16[192,512]{1,0:T(8,128)(2,1)S(1)}, u32[]{:S(2)}, u32[]{:S(2)}) %collective-permute-start.25) | collective-permute-done | bytes 196640 | tf_op jit(solution)/shard_map/ppermute | solution.py:41
  159.2 1.9 %shard_map.99 = bf16[1,4,192,2,1024]{4,3,2,1,0:T(2,128)(2,1)} custom-call(s32[1]{0:T(128)} %bitcast.decoder_ref, bf16[192,512]{1,0:T(8,128)(2,1)S(1)} %copy-done.12, bf16[192,512]{1,0:T(8,128)(2,1)S(1)} %copy-done.16, bf16[192,512]{1,0:T(8,128)(2,1)} %collective-permute-done.24.context_ref, ...), custom_call_target="tpu_custom_call", output_to_operand_aliasing={{}: (4, {})} | custom-call | flops 589824 | bytes 983040 | tf_op jit(solution)/shard_map/pallas_call | solution.py:239
  (89 shorter events, 14.0 us)
Async XLA Ops:
  6.5 73.7 %all-gather.2.cloned.1.call-start = ((), (), s32[]{:S(2)}) async-start(), calls=%async_computation | async-start | bytes 7864320 | tf_op jit(solution)/shard_map/all_gather | solution.py:265
  8.4 17.1 %collective-permute-start.6 = (bf16[128,2048]{1,0:T(8,128)(2,1)S(1)}, bf16[128,2048]{1,0:T(8,128)(2,1)S(1)}, u32[]{:S(2)}, u32[]{:S(2)}) collective-permute-start(bf16[128,2048]{1,0:T(8,128)(2,1)S(1)} %bitcast.7), channel_id=1, source_target_pairs={{0,112},{1,113},{2,114},{3,115},{4,116},{5,117},{6,118},{7,119},{8... | collective-permute-start | bytes 1572872 | tf_op jit(solution)/shard_map/ppermute | solution.py:41
  14.3 14.9 %collective-permute-start.8 = (bf16[128,2048]{1,0:T(8,128)(2,1)S(1)}, bf16[128,2048]{1,0:T(8,128)(2,1)S(1)}, u32[]{:S(2)}, u32[]{:S(2)}) collective-permute-start(bf16[128,2048]{1,0:T(8,128)(2,1)S(1)} %bitcast.8), channel_id=1, source_target_pairs={{0,8},{1,9},{2,10},{3,11},{4,12},{5,13},{6,14},{7,15},{8,0},{9,1},... | collective-permute-start | bytes 1572872 | tf_op jit(solution)/shard_map/ppermute | solution.py:41
  16.6 14.3 %collective-permute-start = (bf16[128,2048]{1,0:T(8,128)(2,1)S(1)}, bf16[128,2048]{1,0:T(8,128)(2,1)S(1)}, u32[]{:S(2)}, u32[]{:S(2)}) collective-permute-start(bf16[128,2048]{1,0:T(8,128)(2,1)S(1)} %bitcast.9), channel_id=1, source_target_pairs={{0,16},{1,17},{2,18},{3,19},{4,20},{5,21},{6,22},{7,23},{8,24},{9,... | collective-permute-start | bytes 1572872 | tf_op jit(solution)/shard_map/ppermute | solution.py:41
  31.0 13.4 %collective-permute-start.2 = (bf16[128,2048]{1,0:T(8,128)(2,1)S(1)}, bf16[128,2048]{1,0:T(8,128)(2,1)S(1)}, u32[]{:S(2)}, u32[]{:S(2)}) collective-permute-start(bf16[128,2048]{1,0:T(8,128)(2,1)S(1)} %collective-permute-done.refs_1_), channel_id=1, source_target_pairs={{0,16},{1,17},{2,18},{3,19},{4,20},{5,21},{6,22},{7,23},{8,24},{9,... | collective-permute-start | bytes 1572872 | tf_op jit(solution)/shard_map/ppermute | solution.py:41
  31.0 16.4 %collective-permute-start.7 = (bf16[128,2048]{1,0:T(8,128)(2,1)S(1)}, bf16[128,2048]{1,0:T(8,128)(2,1)S(1)}, u32[]{:S(2)}, u32[]{:S(2)}) collective-permute-start(bf16[128,2048]{1,0:T(8,128)(2,1)S(1)} %collective-permute-done.6.refs_2_), channel_id=1, source_target_pairs={{0,8},{1,9},{2,10},{3,11},{4,12},{5,13},{6,14},{7,15},{8,0},{9,1},... | collective-permute-start | bytes 1572872 | tf_op jit(solution)/shard_map/ppermute | solution.py:41
  32.2 15.1 %collective-permute-start.9 = (bf16[128,2048]{1,0:T(8,128)(2,1)S(1)}, bf16[128,2048]{1,0:T(8,128)(2,1)S(1)}, u32[]{:S(2)}, u32[]{:S(2)}) collective-permute-start(bf16[128,2048]{1,0:T(8,128)(2,1)S(1)} %collective-permute-done.6.refs_2_), channel_id=1, source_target_pairs={{0,112},{1,113},{2,114},{3,115},{4,116},{5,117},{6,118},{7,119},{8... | collective-permute-start | bytes 1572872 | tf_op jit(solution)/shard_map/ppermute | solution.py:41
  35.4 21.5 %collective-permute-start.1 = (bf16[128,2048]{1,0:T(8,128)(2,1)S(1)}, bf16[128,2048]{1,0:T(8,128)(2,1)S(1)}, u32[]{:S(2)}, u32[]{:S(2)}) collective-permute-start(bf16[128,2048]{1,0:T(8,128)(2,1)S(1)} %collective-permute-done.refs_1_), channel_id=1, source_target_pairs={{0,8},{1,9},{2,10},{3,11},{4,12},{5,13},{6,14},{7,15},{8,0},{9,1},... | collective-permute-start | bytes 1572872 | tf_op jit(solution)/shard_map/ppermute | solution.py:41
  44.3 12.6 %collective-permute-start.3 = (bf16[128,2048]{1,0:T(8,128)(2,1)S(1)}, bf16[128,2048]{1,0:T(8,128)(2,1)S(1)}, u32[]{:S(2)}, u32[]{:S(2)}) collective-permute-start(bf16[128,2048]{1,0:T(8,128)(2,1)S(1)} %collective-permute-done.2.refs_3_), channel_id=1, source_target_pairs={{0,16},{1,17},{2,18},{3,19},{4,20},{5,21},{6,22},{7,23},{8,24},{9,... | collective-permute-start | bytes 1572872 | tf_op jit(solution)/shard_map/ppermute | solution.py:41
  47.3 10.4 %collective-permute-start.10 = (bf16[128,2048]{1,0:T(8,128)(2,1)S(1)}, bf16[128,2048]{1,0:T(8,128)(2,1)S(1)}, u32[]{:S(2)}, u32[]{:S(2)}) collective-permute-start(bf16[128,2048]{1,0:T(8,128)(2,1)S(1)} %collective-permute-done.9.refs_4_), channel_id=1, source_target_pairs={{0,112},{1,113},{2,114},{3,115},{4,116},{5,117},{6,118},{7,119},{8... | collective-permute-start | bytes 1572872 | tf_op jit(solution)/shard_map/ppermute | solution.py:41
  56.9 11.9 %collective-permute-start.4 = (bf16[128,2048]{1,0:T(8,128)(2,1)S(1)}, bf16[128,2048]{1,0:T(8,128)(2,1)}, u32[]{:S(2)}, u32[]{:S(2)}) collective-permute-start(bf16[128,2048]{1,0:T(8,128)(2,1)S(1)} %collective-permute-done.3.refs_0_), channel_id=1, source_target_pairs={{0,16},{1,17},{2,18},{3,19},{4,20},{5,21},{6,22},{7,23},{8,24},{9,... | collective-permute-start | bytes 1572872 | tf_op jit(solution)/shard_map/ppermute | solution.py:41
  57.7 11.0 %collective-permute-start.11 = (bf16[128,2048]{1,0:T(8,128)(2,1)S(1)}, bf16[128,2048]{1,0:T(8,128)(2,1)}, u32[]{:S(2)}, u32[]{:S(2)}) collective-permute-start(bf16[128,2048]{1,0:T(8,128)(2,1)S(1)} %collective-permute-done.7.refs_3_), channel_id=1, source_target_pairs={{0,112},{1,113},{2,114},{3,115},{4,116},{5,117},{6,118},{7,119},{8... | collective-permute-start | bytes 1572872 | tf_op jit(solution)/shard_map/ppermute | solution.py:41
  61.4 10.7 %collective-permute-start.12 = (bf16[128,2048]{1,0:T(8,128)(2,1)S(1)}, bf16[128,2048]{1,0:T(8,128)(2,1)S(1)}, u32[]{:S(2)}, u32[]{:S(2)}) collective-permute-start(bf16[128,2048]{1,0:T(8,128)(2,1)S(1)} %collective-permute-done.3.refs_0_), channel_id=1, source_target_pairs={{0,8},{1,9},{2,10},{3,11},{4,12},{5,13},{6,14},{7,15},{8,0},{9,1},... | collective-permute-start | bytes 1572872 | tf_op jit(solution)/shard_map/ppermute | solution.py:41
  63.7 11.3 %copy-start.24 = (s32[32]{0:T(128)S(1)}, s32[32]{0:T(128)}, u32[]{:S(2)}) copy-start(s32[32]{0:T(128)} %constant.81.clone) | copy-start | bytes 388
  63.7 11.3 %copy-start.25 = (s32[32]{0:T(128)S(1)}, s32[32]{0:T(128)}, u32[]{:S(2)}) copy-start(s32[32]{0:T(128)} %constant.78.clone) | copy-start | bytes 388
  63.7 11.3 %copy-start.26 = (s32[32]{0:T(128)S(1)}, s32[32]{0:T(128)}, u32[]{:S(2)}) copy-start(s32[32]{0:T(128)} %constant.79.clone) | copy-start | bytes 388
  63.7 11.3 %copy-start.23 = (s32[32]{0:T(128)S(1)}, s32[32]{0:T(128)}, u32[]{:S(2)}) copy-start(s32[32]{0:T(128)} %constant.86) | copy-start | bytes 388
  63.7 25.2 %collective-permute-start.16 = (bf16[640,2048]{1,0:T(8,128)(2,1)S(1)}, bf16[640,2048]{1,0:T(8,128)(2,1)}, u32[]{:S(2)}, u32[]{:S(2)}) collective-permute-start(bf16[640,2048]{1,0:T(8,128)(2,1)S(1)} %shard_map.84.refs_3_), channel_id=1, source_target_pairs={{0,4},{1,5},{2,6},{3,7},{4,0},{5,1},{6,2},{7,3},{8,12},{9,13},{10,... | collective-permute-start | bytes 7864328 | tf_op jit(solution)/shard_map/ppermute | solution.py:41
  65.4 14.9 %copy-start.21 = (f32[1,4096]{1,0:T(1,128)S(1)}, f32[1,4096]{1,0:T(1,128)}, u32[]{:S(2)}) copy-start(f32[1,4096]{1,0:T(1,128)} %gain_ref.1) | copy-start | bytes 49156
  65.4 25.0 %collective-permute-start.17 = (bf16[640,2048]{1,0:T(8,128)(2,1)}, bf16[640,2048]{1,0:T(8,128)(2,1)}, u32[]{:S(2)}, u32[]{:S(2)}) collective-permute-start(bf16[640,2048]{1,0:T(8,128)(2,1)} %shard_map.85.refs_5_), channel_id=1, source_target_pairs={{0,4},{1,5},{2,6},{3,7},{4,0},{5,1},{6,2},{7,3},{8,12},{9,13},{10,... | collective-permute-start | bytes 7864328 | tf_op jit(solution)/shard_map/ppermute | solution.py:41
  68.8 18.0 %collective-permute-start.5 = (bf16[128,2048]{1,0:T(8,128)(2,1)S(1)}, bf16[128,2048]{1,0:T(8,128)(2,1)}, u32[]{:S(2)}, u32[]{:S(2)}) collective-permute-start(bf16[128,2048]{1,0:T(8,128)(2,1)S(1)} %collective-permute-done.1.refs_4_), channel_id=1, source_target_pairs={{0,16},{1,17},{2,18},{3,19},{4,20},{5,21},{6,22},{7,23},{8,24},{9,... | collective-permute-start | bytes 1572872 | tf_op jit(solution)/shard_map/ppermute | solution.py:41
  73.0 14.0 %collective-permute-start.13 = (bf16[128,2048]{1,0:T(8,128)(2,1)}, bf16[128,2048]{1,0:T(8,128)(2,1)}, u32[]{:S(2)}, u32[]{:S(2)}) collective-permute-start(bf16[128,2048]{1,0:T(8,128)(2,1)} %collective-permute-done.11.refs_1_), channel_id=1, source_target_pairs={{0,112},{1,113},{2,114},{3,115},{4,116},{5,117},{6,118},{7,119},{8... | collective-permute-start | bytes 1572872 | tf_op jit(solution)/shard_map/ppermute | solution.py:41
  73.1 13.8 %collective-permute-start.14 = (bf16[128,2048]{1,0:T(8,128)(2,1)}, bf16[128,2048]{1,0:T(8,128)(2,1)}, u32[]{:S(2)}, u32[]{:S(2)}) collective-permute-start(bf16[128,2048]{1,0:T(8,128)(2,1)} %collective-permute-done.4.refs_0_), channel_id=1, source_target_pairs={{0,8},{1,9},{2,10},{3,11},{4,12},{5,13},{6,14},{7,15},{8,0},{9,1},... | collective-permute-start | bytes 1572872 | tf_op jit(solution)/shard_map/ppermute | solution.py:41
  86.8 3.5 %collective-permute-start.18 = (bf16[384,2048]{1,0:T(8,128)(2,1)S(1)}, bf16[384,2048]{1,0:T(8,128)(2,1)S(1)}, u32[]{:S(2)}, u32[]{:S(2)}) collective-permute-start(bf16[384,2048]{1,0:T(8,128)(2,1)S(1)} %copy-done.1), channel_id=1, source_target_pairs={{0,4},{1,5},{2,6},{3,7},{4,0},{5,1},{6,2},{7,3},{8,12},{9,13},{10,... | collective-permute-start | bytes 4718600 | tf_op jit(solution)/shard_map/ppermute | solution.py:41
  88.4 4.2 %collective-permute-start.15 = (bf16[384,2048]{1,0:T(8,128)(2,1)S(1)}, bf16[384,2048]{1,0:T(8,128)(2,1)S(1)}, u32[]{:S(2)}, u32[]{:S(2)}) collective-permute-start(bf16[384,2048]{1,0:T(8,128)(2,1)S(1)} %shard_map.83.refs_1_), channel_id=1, source_target_pairs={{0,4},{1,5},{2,6},{3,7},{4,0},{5,1},{6,2},{7,3},{8,12},{9,13},{10,... | collective-permute-start | bytes 4718600 | tf_op jit(solution)/shard_map/ppermute | solution.py:41
  101.9 26.3 %copy-start.5 = (bf16[192,1024]{1,0:T(8,128)(2,1)}, bf16[192,1024]{1,0:T(8,128)(2,1)S(1)}, u32[]{:S(2)}) copy-start(bf16[192,1024]{1,0:T(8,128)(2,1)S(1)} %get-tuple-element.45.k_ref.front_ref) | copy-start | bytes 1179652
  101.9 30.1 %copy-start.3 = (bf16[192,1024]{1,0:T(8,128)(2,1)}, bf16[192,1024]{1,0:T(8,128)(2,1)S(1)}, u32[]{:S(2)}) copy-start(bf16[192,1024]{1,0:T(8,128)(2,1)S(1)} %get-tuple-element.39.k_ref.front_ref) | copy-start | bytes 1179652
  101.9 36.4 %copy-start.13 = (bf16[192,512]{1,0:T(8,128)(2,1)}, bf16[192,512]{1,0:T(8,128)(2,1)S(1)}, u32[]{:S(2)}) copy-start(bf16[192,512]{1,0:T(8,128)(2,1)S(1)} %get-tuple-element.38.k_ref.front_ref) | copy-start | bytes 589828
  101.9 40.4 %copy-start.11 = (bf16[192,512]{1,0:T(8,128)(2,1)}, bf16[192,512]{1,0:T(8,128)(2,1)S(1)}, u32[]{:S(2)}) copy-start(bf16[192,512]{1,0:T(8,128)(2,1)S(1)} %get-tuple-element.33.k_ref.front_ref) | copy-start | bytes 589828
  101.9 13.7 %collective-permute-start.19 = (bf16[192,1024]{1,0:T(8,128)(2,1)S(1)}, bf16[192,1024]{1,0:T(8,128)(2,1)S(1)}, u32[]{:S(2)}, u32[]{:S(2)}) collective-permute-start(bf16[192,1024]{1,0:T(8,128)(2,1)S(1)} %get-tuple-element.34.k_ref.front_ref), channel_id=1, source_target_pairs={{128,0},{129,1},{130,2},{131,3},{132,4},{133,5},{134,6},{135,7},{1... | collective-permute-start | bytes 1179656 | tf_op jit(solution)/shard_map/ppermute | solution.py:41
  104.4 17.9 %collective-permute-start.23 = (bf16[192,1024]{1,0:T(8,128)(2,1)S(1)}, bf16[192,1024]{1,0:T(8,128)(2,1)S(1)}, u32[]{:S(2)}, u32[]{:S(2)}) collective-permute-start(bf16[192,1024]{1,0:T(8,128)(2,1)S(1)} %get-tuple-element.45.k_ref.front_ref), channel_id=1, source_target_pairs={{128,0},{129,1},{130,2},{131,3},{132,4},{133,5},{134,6},{135,7},{1... | collective-permute-start | bytes 1179656 | tf_op jit(solution)/shard_map/ppermute | solution.py:41
  105.7 26.3 %collective-permute-start.22 = (bf16[192,1024]{1,0:T(8,128)(2,1)S(1)}, bf16[192,1024]{1,0:T(8,128)(2,1)S(1)}, u32[]{:S(2)}, u32[]{:S(2)}) collective-permute-start(bf16[192,1024]{1,0:T(8,128)(2,1)S(1)} %get-tuple-element.39.k_ref.front_ref), channel_id=1, source_target_pairs={{128,0},{129,1},{130,2},{131,3},{132,4},{133,5},{134,6},{135,7},{1... | collective-permute-start | bytes 1179656 | tf_op jit(solution)/shard_map/ppermute | solution.py:41
  107.0 35.2 %collective-permute-start.20 = (bf16[192,512]{1,0:T(8,128)(2,1)S(1)}, bf16[192,512]{1,0:T(8,128)(2,1)S(1)}, u32[]{:S(2)}, u32[]{:S(2)}) collective-permute-start(bf16[192,512]{1,0:T(8,128)(2,1)S(1)} %get-tuple-element.33.k_ref.front_ref), channel_id=1, source_target_pairs={{128,0},{129,1},{130,2},{131,3},{132,4},{133,5},{134,6},{135,7},{1... | collective-permute-start | bytes 589832 | tf_op jit(solution)/shard_map/ppermute | solution.py:41
  108.3 7.2 %copy-start.22 = (s32[4,1]{0,1:T(1,128)S(1)}, s32[4,1]{0,1:T(1,128)}, u32[]{:S(2)}) copy-start(s32[4,1]{0,1:T(1,128)} %param.11) | copy-start | bytes 52
  108.4 29.9 %collective-permute-start.21 = (bf16[192,512]{1,0:T(8,128)(2,1)S(1)}, bf16[192,512]{1,0:T(8,128)(2,1)S(1)}, u32[]{:S(2)}, u32[]{:S(2)}) collective-permute-start(bf16[192,512]{1,0:T(8,128)(2,1)S(1)} %get-tuple-element.38.k_ref.front_ref), channel_id=1, source_target_pairs={{128,0},{129,1},{130,2},{131,3},{132,4},{133,5},{134,6},{135,7},{1... | collective-permute-start | bytes 589832 | tf_op jit(solution)/shard_map/ppermute | solution.py:41
  115.6 12.7 %copy-start.7 = (bf16[192,1024]{1,0:T(8,128)(2,1)}, bf16[192,1024]{1,0:T(8,128)(2,1)S(1)}, u32[]{:S(2)}) copy-start(bf16[192,1024]{1,0:T(8,128)(2,1)S(1)} %get-tuple-element.42.v_ref.back_ref) | copy-start | bytes 1179652
  118.8 27.3 %collective-permute-start.28 = (bf16[192,1024]{1,0:T(8,128)(2,1)}, bf16[192,1024]{1,0:T(8,128)(2,1)}, u32[]{:S(2)}, u32[]{:S(2)}) collective-permute-start(bf16[192,1024]{1,0:T(8,128)(2,1)} %shard_map.89), channel_id=1, source_target_pairs={{0,128},{1,129},{2,130},{3,131},{4,132},{5,133},{6,134},{7,135},{8... | collective-permute-start | bytes 1179656 | tf_op jit(solution)/shard_map/ppermute | solution.py:41
  128.2 10.1 %copy-start.9 = (bf16[192,1024]{1,0:T(8,128)(2,1)}, bf16[192,1024]{1,0:T(8,128)(2,1)S(1)}, u32[]{:S(2)}) copy-start(bf16[192,1024]{1,0:T(8,128)(2,1)S(1)} %get-tuple-element.43.v_ref.back_ref) | copy-start | bytes 1179652
  128.2 16.6 %copy-start.15 = (bf16[192,512]{1,0:T(8,128)(2,1)}, bf16[192,512]{1,0:T(8,128)(2,1)S(1)}, u32[]{:S(2)}) copy-start(bf16[192,512]{1,0:T(8,128)(2,1)S(1)} %get-tuple-element.37.v_ref.back_ref) | copy-start | bytes 589828
  128.2 16.6 %copy-start.17 = (bf16[192,512]{1,0:T(8,128)(2,1)}, bf16[192,512]{1,0:T(8,128)(2,1)S(1)}, u32[]{:S(2)}) copy-start(bf16[192,512]{1,0:T(8,128)(2,1)S(1)} %get-tuple-element.44.v_ref.back_ref) | copy-start | bytes 589828
  130.7 17.5 %collective-permute-start.27 = (bf16[192,1024]{1,0:T(8,128)(2,1)S(1)}, bf16[192,1024]{1,0:T(8,128)(2,1)S(1)}, u32[]{:S(2)}, u32[]{:S(2)}) collective-permute-start(bf16[192,1024]{1,0:T(8,128)(2,1)S(1)} %shard_map.91), channel_id=1, source_target_pairs={{0,128},{1,129},{2,130},{3,131},{4,132},{5,133},{6,134},{7,135},{8... | collective-permute-start | bytes 1179656 | tf_op jit(solution)/shard_map/ppermute | solution.py:41
  134.5 18.6 %collective-permute-start.26 = (bf16[192,1024]{1,0:T(8,128)(2,1)S(1)}, bf16[192,1024]{1,0:T(8,128)(2,1)S(1)}, u32[]{:S(2)}, u32[]{:S(2)}) collective-permute-start(bf16[192,1024]{1,0:T(8,128)(2,1)S(1)} %shard_map.92), channel_id=1, source_target_pairs={{0,128},{1,129},{2,130},{3,131},{4,132},{5,133},{6,134},{7,135},{8... | collective-permute-start | bytes 1179656 | tf_op jit(solution)/shard_map/ppermute | solution.py:41
  140.8 7.4 %copy-start.6 = (bf16[192,1024]{1,0:T(8,128)(2,1)S(1)}, bf16[192,1024]{1,0:T(8,128)(2,1)}, u32[]{:S(2)}) copy-start(bf16[192,1024]{1,0:T(8,128)(2,1)} %copy-done.5) | copy-start | bytes 1179652
  140.8 7.4 %copy-start.8 = (bf16[192,1024]{1,0:T(8,128)(2,1)S(1)}, bf16[192,1024]{1,0:T(8,128)(2,1)}, u32[]{:S(2)}) copy-start(bf16[192,1024]{1,0:T(8,128)(2,1)} %copy-done.7) | copy-start | bytes 1179652
  140.8 16.1 %collective-permute-start.25 = (bf16[192,512]{1,0:T(8,128)(2,1)}, bf16[192,512]{1,0:T(8,128)(2,1)S(1)}, u32[]{:S(2)}, u32[]{:S(2)}) collective-permute-start(bf16[192,512]{1,0:T(8,128)(2,1)} %shard_map.93), channel_id=1, source_target_pairs={{0,128},{1,129},{2,130},{3,131},{4,132},{5,133},{6,134},{7,135},{8... | collective-permute-start | bytes 589832 | tf_op jit(solution)/shard_map/ppermute | solution.py:41
  144.8 14.4 %collective-permute-start.24 = (bf16[192,512]{1,0:T(8,128)(2,1)}, bf16[192,512]{1,0:T(8,128)(2,1)}, u32[]{:S(2)}, u32[]{:S(2)}) collective-permute-start(bf16[192,512]{1,0:T(8,128)(2,1)} %shard_map.94), channel_id=1, source_target_pairs={{0,128},{1,129},{2,130},{3,131},{4,132},{5,133},{6,134},{7,135},{8... | collective-permute-start | bytes 589832 | tf_op jit(solution)/shard_map/ppermute | solution.py:41
  149.5 7.5 %copy-start.14 = (bf16[192,512]{1,0:T(8,128)(2,1)S(1)}, bf16[192,512]{1,0:T(8,128)(2,1)}, u32[]{:S(2)}) copy-start(bf16[192,512]{1,0:T(8,128)(2,1)} %copy-done.13) | copy-start | bytes 589828
  149.5 7.5 %copy-start.18 = (bf16[192,512]{1,0:T(8,128)(2,1)S(1)}, bf16[192,512]{1,0:T(8,128)(2,1)}, u32[]{:S(2)}) copy-start(bf16[192,512]{1,0:T(8,128)(2,1)} %copy-done.17) | copy-start | bytes 589828
  (9 other events, 29.3 us)
Sparse Core Ops, SparseCore 0:
  9.2 71.0 all-gather.1
